TPU v7x, 512 devices: a whole 4x8x8 slice. The times are simulated.
512 devices in a mesh: row: 32 (over z, x), col: 16 (over y, core).
Axes of the slice: x: 4, y: 8, z: 8, core: 2. Of those that a mesh axis runs over, the one named last changes fastest.
Arguments:
- density: float32 [32, 256, 2048], P(None, 'row', 'col'), may hold values from 0 to 1
- threshold_index: int32 [3], replicated, may hold values from 4 to 12
- channel_width: int32 [30], replicated, may hold values from 0 to 9
- sigma_table: float32 [10], replicated, may hold values from 1.5 to 64
Outputs:
- compliance: float32 [30], replicated
- sensitivity: float32 [32, 256, 2048], P(None, 'row', 'col')
All inputs are finite; a program needn't handle non-finite values.
Results may differ from a plain program's by a relative error of at most 0.0013.
Values may be sent and summed in bfloat16 or wider, within the bound.
No kernel may reach another device: no remote copies, remote signals or barrier semaphores. Data moves between devices by JAX's collectives and lax.ppermute only.
A program may use at most 64 MiB of HBM per device.

v0:
```python
from functools import partial

import jax
import jax.numpy as jnp
from jax import lax
from jax.sharding import PartitionSpec as P

VARIANTS = 3
WIDTHS = 10
CHANNELS = 30
HALF = 128


sharpness = 8.0
spread_floor = 0.0001


def extended(x, sides, width):
    for axis, dim in sides:
        size, length = (lax.axis_size(axis), x.shape[dim])
        up = [(i, (i + 1) % size) for i in range(size - 1)]
        down = [(j, i) for i, j in up]
        last = lax.slice_in_dim(x, length - width, length, axis=dim)
        first = lax.slice_in_dim(x, 0, width, axis=dim)
        before = lax.ppermute(last, axis, up)
        after = lax.ppermute(first, axis, down)
        x = jnp.concatenate([before, x, after], axis=dim)
    return x


def project(density, threshold_index):
    levels = threshold_index.astype(jnp.float32) / 16.0
    levels = levels.reshape((-1,) + (1,) * density.ndim)
    low = jnp.tanh(sharpness * levels)
    high = jnp.tanh(sharpness * (1.0 - levels))
    return (low + jnp.tanh(sharpness * (density - levels))) / (low + high)


def slope(density, threshold_index):
    levels = threshold_index.astype(jnp.float32) / 16.0
    levels = levels.reshape((-1,) + (1,) * density.ndim)
    low = jnp.tanh(sharpness * levels)
    high = jnp.tanh(sharpness * (1.0 - levels))
    inner = jnp.tanh(sharpness * (density - levels))
    return sharpness * (1.0 - inner * inner) / (low + high)


def gauss_band(width_value, num_rows, num_cols, offset):
    row_ids = lax.broadcasted_iota(jnp.float32, (num_rows, num_cols), 0)
    col_ids = lax.broadcasted_iota(jnp.float32, (num_rows, num_cols), 1)
    offsets = row_ids - col_ids - offset
    tap_axis = jnp.arange(-HALF, HALF + 1).astype(jnp.float32)
    inverse = 1.0 / jnp.sum(jnp.exp(-tap_axis * tap_axis / (2.0 * width_value * width_value)))
    values = jnp.exp(-offsets * offsets / (2.0 * width_value * width_value)) * inverse
    return jnp.where(jnp.abs(offsets) <= HALF, values, 0.0).astype(jnp.bfloat16)


def width_of(sigma_table, channel_width, index):
    slot = jnp.sum(jnp.where(jnp.arange(channel_width.shape[0]) == index, channel_width, 0))
    return jnp.sum(jnp.where(jnp.arange(sigma_table.shape[0]) == slot, sigma_table, 0.0))


def along_x(sigma_table, channel_width, wide, index):
    variant = index // WIDTHS
    cols_out = wide.shape[-1] - 2 * HALF
    matrix = gauss_band(
        width_of(sigma_table, channel_width, index), wide.shape[-1], cols_out, float(HALF)
    )
    source = lax.dynamic_index_in_dim(wide, variant, 0, keepdims=False)
    return jnp.einsum("...j,ji->...i", source, matrix, preferred_element_type=jnp.float32).astype(
        jnp.bfloat16
    )


def per_device(density, threshold_index, channel_width, sigma_table):
    channel_ids = jnp.arange(CHANNELS, dtype=jnp.int32)
    smooth_x = partial(along_x, sigma_table, channel_width)
    wide_density = extended(density, (("col", 2),), HALF)
    wide = project(wide_density, threshold_index).astype(jnp.bfloat16)
    panels = lax.map(partial(smooth_x, wide), channel_ids)
    middle = wide[..., HALF : wide.shape[-1] - HALF]
    panels, variants = (
        lax.all_to_all(panels, "row", split_axis=1, concat_axis=2, tiled=True),
        lax.all_to_all(middle, "row", split_axis=1, concat_axis=2, tiled=True),
    )
    length = variants.shape[2]

    def along_y(index):
        variant = index // WIDTHS
        matrix = gauss_band(width_of(sigma_table, channel_width, index), length, length, 0.0)
        source = lax.dynamic_index_in_dim(panels, index, 0, keepdims=False)
        field = jnp.einsum("zyx,yw->zwx", source, matrix, preferred_element_type=jnp.float32)
        owner = lax.dynamic_index_in_dim(variants, variant, 0, keepdims=False).astype(jnp.float32)
        return (field, jnp.sum(owner * field))

    smoothed, partials = lax.map(along_y, channel_ids)
    cell_count = (
        lax.axis_size("row") * lax.axis_size("col") * variants.shape[1] * length * variants.shape[3]
    )
    compliance = lax.psum(partials, ("row", "col")) / cell_count
    mean_value = jnp.mean(compliance)
    spread = jnp.sqrt(jnp.mean((compliance - mean_value) ** 2) + spread_floor)
    weights = (1.0 + (compliance - mean_value) / spread) / CHANNELS
    member = (
        lax.broadcasted_iota(jnp.int32, (VARIANTS, CHANNELS), 1) // WIDTHS
        == lax.broadcasted_iota(jnp.int32, (VARIANTS, CHANNELS), 0)
    ).astype(jnp.float32)
    combined = jnp.einsum(
        "vc,czyx->vzyx",
        member * (2.0 * weights)[None, :],
        smoothed,
        precision=lax.Precision.HIGHEST,
    )
    returned = lax.all_to_all(combined, "row", split_axis=2, concat_axis=1, tiled=True)
    sensitivity = jnp.sum(slope(density, threshold_index) * returned, axis=0)
    return (compliance, sensitivity)


def solution(mesh):
    in_specs = (P(None, "row", "col"), P(), P(), P())
    out_specs = (P(), P(None, "row", "col"))
    return jax.shard_map(
        per_device, mesh=mesh, in_specs=in_specs, out_specs=out_specs, check_vma=False
    )
```

profile of v0, /device:TPU:1, one launch (start us, length us, event | category | flops | bytes accessed | tf_op | source)
XLA Modules:
  0.0 858.4 jit_solution(10198214440540660656)
XLA Ops:
  0.6 4.7 collective-permute-start
  5.4 5.5 collective-permute-start.1
  14.0 12.7 %all-to-all-start.1 = ((bf16[3,32,8,128]{3,2,0,1:T(8,128)(2,1)}), bf16[3,32,8,128]{3,2,0,1:T(8,128)(2,1)S(1)}, u32[]{:S(2)}, u32[]{:S(2)}) async-start(bf16[3,32,8,128]{3,2,0,1:T(8,128)(2,1)} %slice.4), calls=%async_computation.1 | async-start | bytes 393216 | tf_op jit(solution)/shard_map/all_to_all | solution.py:84
  26.7 259.6 %while.26 = (s32[]{:T(128)}, bf16[30,32,8,128]{3,2,0,1:T(8,128)(2,1)}, s32[30]{0:T(128)S(1)}, bf16[3,32,8,384]{3,2,0,1:T(8,128)(2,1)S(1)}, s32[30]{0:T(128)S(1)}...) while((s32[]{:T(128)}, ...), condition=%wide.region_4.5_spmd, body=%wide.region_0.4_spmd.sunk | while | flops 25691788 | bytes 263137 | solution.py:80
  286.3 9.2 %all-to-all-start = ((bf16[30,32,8,128]{3,2,0,1:T(8,128)(2,1)}), bf16[30,32,8,128]{3,2,0,1:T(8,128)(2,1)S(1)}, u32[]{:S(2)}, u32[]{:S(2)}) async-start(bf16[30,32,8,128]{3,2,0,1:T(8,128)(2,1)} %get-tuple-element.184), calls=%async_computation | async-start | bytes 3932160 | tf_op jit(solution)/shard_map/all_to_all | solution.py:83
  295.6 45.5 %all-to-all-done = bf16[30,32,8,128]{3,2,0,1:T(8,128)(2,1)S(1)} async-done(((bf16[30,32,8,128]{3,2,0,1:T(8,128)(2,1)}), bf16[30,32,8,128]{3,2,0,1:T(8,128)(2,1)S(1)}, u32[]{:S(2)}, u32[]{:S(2)}) %all-to-all-start) | async-done | bytes 1966112 | tf_op jit(solution)/shard_map/all_to_all | solution.py:83
  341.1 1.8 copy.40
  343.0 388.2 %while.27 = (s32[]{:T(128)}, f32[30,1,256,128]{3,2,1,0:T(8,128)}, f32[30]{0:T(128)S(1)}, s32[30]{0:T(128)S(1)}, s32[30]{0:T(128)S(1)}, /*index=5*/f32[10]{0:T(12...) while((s32[]{:T(128)}, f32[30,1,256,128]{3,2,1,0:T(8,128)}, ...), condition=%wide.region_10.11_spmd, body=%wide.region_5.10_spmd.sunk | while | flops 17467012 | bytes 525359 | solution.py:96
  345.5 1.4 fusion.78
  350.7 1.8 bitcast_dynamic-update-slice_fusion.2
  358.4 1.4 fusion.78
  363.7 1.8 bitcast_dynamic-update-slice_fusion.2
  371.4 1.4 fusion.78
  376.6 1.8 bitcast_dynamic-update-slice_fusion.2
  384.3 1.4 fusion.78
  389.6 1.8 bitcast_dynamic-update-slice_fusion.2
  397.3 1.4 fusion.78
  402.5 1.8 bitcast_dynamic-update-slice_fusion.2
  410.2 1.4 fusion.78
  415.5 1.8 bitcast_dynamic-update-slice_fusion.2
  423.2 1.4 fusion.78
  428.4 1.8 bitcast_dynamic-update-slice_fusion.2
  441.3 1.8 bitcast_dynamic-update-slice_fusion.2
  454.3 1.8 bitcast_dynamic-update-slice_fusion.2
  467.2 1.8 bitcast_dynamic-update-slice_fusion.2
  480.2 1.8 bitcast_dynamic-update-slice_fusion.2
  493.1 1.8 bitcast_dynamic-update-slice_fusion.2
  506.1 1.8 bitcast_dynamic-update-slice_fusion.2
  519.0 1.8 bitcast_dynamic-update-slice_fusion.2
  531.9 1.8 bitcast_dynamic-update-slice_fusion.2
  544.9 1.8 bitcast_dynamic-update-slice_fusion.2
  557.8 1.8 bitcast_dynamic-update-slice_fusion.2
  570.8 1.8 bitcast_dynamic-update-slice_fusion.2
  583.7 1.8 bitcast_dynamic-update-slice_fusion.2
  596.6 1.8 bitcast_dynamic-update-slice_fusion.2
  609.6 1.8 bitcast_dynamic-update-slice_fusion.2
  622.5 1.8 bitcast_dynamic-update-slice_fusion.2
  635.5 1.8 bitcast_dynamic-update-slice_fusion.2
  648.4 1.8 bitcast_dynamic-update-slice_fusion.2
  661.3 1.8 bitcast_dynamic-update-slice_fusion.2
  674.3 1.8 bitcast_dynamic-update-slice_fusion.2
  687.2 1.8 bitcast_dynamic-update-slice_fusion.2
  700.2 1.8 bitcast_dynamic-update-slice_fusion.2
  713.1 1.8 bitcast_dynamic-update-slice_fusion.2
  726.0 1.8 bitcast_dynamic-update-slice_fusion.2
  731.2 98.4 %psum.7 = f32[30]{0:T(128)S(1)} all-reduce(f32[30]{0:T(128)S(1)} %get-tuple-element.185), channel_id=1, replica_groups=mesh['row'=32,'col'=16] {'row','col'}, use_global_device_ids=true, to_apply=%region_11.12 | all-reduce | flops 30 | bytes 240 | tf_op jit(solution)/shard_map/psum | solution.py:100
  832.2 6.3 fusion.49
  839.0 18.6 %all_to_all.33 = f32[3,1,256,128]{3,1,0,2:T(1,128)S(1)} all-to-all(f32[3,1,256,128]{3,1,0,2:T(1,128)S(1)} %copy.26), channel_id=1, replica_groups=mesh['row'=32,'col'=16] {'row'}, dimensions={2} | all-to-all | bytes 786432 | tf_op jit(solution)/shard_map/all_to_all | solution.py:114
  (351 shorter events, 296.6 us)
Async XLA Ops:
  0.6 26.1 %copy-start.2 = (s32[30]{0:T(128)S(1)}, s32[30]{0:T(128)}, u32[]{:S(2)}) copy-start(s32[30]{0:T(128)} %param.10) | copy-start | bytes 364
  0.6 26.1 %copy-start.3 = (f32[10]{0:T(128)S(1)}, f32[10]{0:T(128)}, u32[]{:S(2)}) copy-start(f32[10]{0:T(128)} %param.11) | copy-start | bytes 124
  0.6 10.9 %collective-permute-start = (f32[32,8,128]{2,1,0:T(8,128)}, f32[32,8,128]{2,1,0:T(8,128)S(1)}, u32[]{:S(2)}, u32[]{:S(2)}) collective-permute-start(f32[32,8,128]{2,1,0:T(8,128)} %param.8), channel_id=1, source_target_pairs={{0,1},{1,2},{2,3},{3,4},{4,5},{5,6},{6,7},{7,8},{8,9},{9,10},{10,1... | collective-permute-start | bytes 393224 | tf_op jit(solution)/shard_map/ppermute | solution.py:25
  5.4 6.7 collective-permute-start.1
  14.0 272.3 %all-to-all-start.1 = ((bf16[3,32,8,128]{3,2,0,1:T(8,128)(2,1)}), bf16[3,32,8,128]{3,2,0,1:T(8,128)(2,1)S(1)}, u32[]{:S(2)}, u32[]{:S(2)}) async-start(bf16[3,32,8,128]{3,2,0,1:T(8,128)(2,1)} %slice.4), calls=%async_computation.1 | async-start | bytes 393216 | tf_op jit(solution)/shard_map/all_to_all | solution.py:84
  286.3 54.8 %all-to-all-start = ((bf16[30,32,8,128]{3,2,0,1:T(8,128)(2,1)}), bf16[30,32,8,128]{3,2,0,1:T(8,128)(2,1)S(1)}, u32[]{:S(2)}, u32[]{:S(2)}) async-start(bf16[30,32,8,128]{3,2,0,1:T(8,128)(2,1)} %get-tuple-element.184), calls=%async_computation | async-start | bytes 3932160 | tf_op jit(solution)/shard_map/all_to_all | solution.py:83
  830.2 8.3 copy-start.1
  832.2 25.4 %copy-start = (f32[32,8,128]{2,1,0:T(8,128)S(1)}, f32[32,8,128]{2,1,0:T(8,128)}, u32[]{:S(2)}) copy-start(f32[32,8,128]{2,1,0:T(8,128)} %param.8) | copy-start | bytes 393220
where the time goes:
time: 866 us; the launch traced here: 858 us
  loops' own time  293 us (34%)
  other arithmetic  219 us (25%)
  blocking collectives  117 us (14%)
  matrix products  89.1 us (10%)
  local copies, waits for them, and re-layouts  60.6 us (7%)
  waiting for transfers between devices  46 us (5%)
  starting transfers between devices  32.1 us (4%)
    another operation x1, loops' own time, per_device(): smoothed, partials = lax.map(along_y, channel_ids)  174 us
    another operation x1, loops' own time, per_device(): panels = lax.map(partial(smooth_x, wide), channel_ids)  119 us
    psum x1, blocking collectives, per_device(): compliance = lax.psum(partials, ('row', 'col')) / cell_count  98.4 us
    reduce_sum x60, other arithmetic, width_of(): jnp.sum(jnp.where(jnp.arange(channel_width.shape[0]) == index, channel_wi...  80.9 us
    reduce_sum x60, other arithmetic, width_of(): jnp.sum(jnp.where(jnp.arange(sigma_table.shape[0]) == slot, sigma_table,...  75.4 us
    dot_general x30, matrix products, along_y(): jnp.einsum('zyx,yw->zwx', source, matrix, preferred_element_type=jnp.floa...  54.6 us
    all_to_all x1, waiting for transfers between devices, per_device(): lax.all_to_all(panels, 'row', split_axis=1, concat_axis=2, tiled=True)  45.5 us
    reduce_sum x60, other arithmetic, gauss_band(): jnp.sum(jnp.exp(-tap_axis * tap_axis / (2.0 * width_value * width_value)))  39.1 us
  transfers between devices with their start and end apart: 4, of which 2 were waited for; matrix products, arithmetic and copies ran while one was open for 16% of the time, Pallas kernels for 0%

commit v1 on v0

v1 whole, which is shorter than its diff:
```python
import jax
import jax.numpy as jnp
from jax import lax
from jax.experimental import pallas as pl
from jax.experimental.pallas import tpu as pltpu
from jax.sharding import PartitionSpec as P

VARIANTS = 3
WIDTHS = 10
CHANNELS = 30
HALF = 128
SHARPNESS = 8.0
SPREAD_FLOOR = 0.0001

F32 = jnp.float32
BF16 = jnp.bfloat16
VMEM = pl.BlockSpec(memory_space=pltpu.VMEM)
SMEM = pl.BlockSpec(memory_space=pltpu.SMEM)
MIB = 1024 * 1024


def bands_kernel(sigma_ref, width_ref, xt_ref, y_ref, member_ref):
    row = lax.broadcasted_iota(jnp.int32, (HALF, HALF), 0)
    col = lax.broadcasted_iota(jnp.int32, (HALF, HALF), 1)
    gap = col - row
    gap_f = gap.astype(F32)
    squares = ((gap_f - HALF) ** 2, gap_f * gap_f, (gap_f + HALF) ** 2)
    masks = (gap >= 0, None, gap <= 0)
    taps = lax.broadcasted_iota(jnp.int32, (1, HALF), 1).astype(F32) + 1.0
    for w in range(WIDTHS):
        sigma = jnp.full((1, HALF), sigma_ref[w], F32)
        scale = -1.0 / (2.0 * sigma * sigma)
        total = 1.0 + 2.0 * jnp.sum(jnp.exp(taps * taps * scale), axis=1, keepdims=True)
        inverse = 1.0 / total
        blocks = []
        for square, mask in zip(squares, masks):
            value = jnp.exp(square * scale) * inverse
            if mask is not None:
                value = jnp.where(mask, value, 0.0)
            blocks.append(value.astype(BF16))
        before, middle, after = blocks
        rows = slice(w * HALF, (w + 1) * HALF)
        xt_ref[rows, 0:HALF] = before
        xt_ref[rows, HALF : 2 * HALF] = middle
        xt_ref[rows, 2 * HALF : 3 * HALF] = after
        y_ref[w, 0:HALF, 0:HALF] = middle
        y_ref[w, 0:HALF, HALF : 2 * HALF] = after
        y_ref[w, HALF : 2 * HALF, 0:HALF] = before
        y_ref[w, HALF : 2 * HALF, HALF : 2 * HALF] = middle
    lane = lax.broadcasted_iota(jnp.int32, (1, 128), 1)
    for c in range(CHANNELS):
        pair = (c // WIDTHS) * WIDTHS + width_ref[c]
        member_ref[c : c + 1, :] = (lane == pair).astype(F32)
    member_ref[CHANNELS:32, :] = jnp.zeros((32 - CHANNELS, 128), F32)


def column_to_row(column):
    rows = column.shape[0]
    at = lax.broadcasted_iota(jnp.int32, (rows, 128), 0) == lax.broadcasted_iota(jnp.int32, (rows, 128), 1)
    return jnp.sum(jnp.where(at, jnp.broadcast_to(column, (rows, 128)), 0.0), axis=0, keepdims=True)


def smooth_kernel(index_ref, left_ref, own_ref, right_ref, xt_ref, y_ref, t_ref, s_ref, part_ref, p_ref, own_p_ref, a_ref, rows_ref):
    ny = own_ref.shape[0]
    sides = (left_ref[...].T, own_ref[...].T, right_ref[...].T)
    for v in range(VARIANTS):
        level = jnp.full((1, ny), index_ref[v].astype(F32) * (1.0 / 16.0), F32)
        low = jnp.tanh(SHARPNESS * level)
        high = jnp.tanh(SHARPNESS * (1.0 - level))
        inverse = 1.0 / (low + high)
        for b, side in enumerate(sides):
            inner = jnp.tanh(SHARPNESS * (side - level))
            value = ((low + inner) * inverse).astype(BF16)
            p_ref[b * HALF : (b + 1) * HALF, :] = value
            if b == 1:
                own_p_ref[v] = value.astype(F32)
                s_ref[v] = SHARPNESS * (1.0 - inner * inner) * inverse
        along = jnp.dot(xt_ref[...], p_ref[...], preferred_element_type=F32).astype(BF16)
        a_ref[:, v * HALF : (v + 1) * HALF, :] = along.reshape(WIDTHS, HALF, ny)
    rows_ref[...] = jnp.zeros_like(rows_ref)

    def per_width(w, carry):
        field = jnp.dot(a_ref[w], y_ref[w], preferred_element_type=F32)
        t_ref[w] = field
        for v in range(VARIANTS):
            product = field[v * HALF : (v + 1) * HALF, :] * own_p_ref[v]
            line = jnp.sum(product, axis=0, keepdims=True)
            rows_ref[pl.ds(v * WIDTHS + w, 1), :] = line[:, 0:128] + line[:, 128:256]
        return carry

    lax.fori_loop(0, WIDTHS, per_width, 0)
    sums = column_to_row(jnp.sum(rows_ref[...], axis=1, keepdims=True))
    part_ref[...] = jnp.broadcast_to(sums.reshape(1, 1, 128), part_ref.shape)


def gather_kernel(in_ref, out_ref):
    total = jnp.sum(in_ref[...], axis=0, keepdims=True)
    out_ref[...] = jnp.broadcast_to(total, out_ref.shape)


def combine_kernel(cells, sums_ref, member_ref, t_ref, s_ref, compliance_ref, out_ref):
    pairs = jnp.sum(sums_ref[...], axis=0) * (1.0 / cells)
    member = member_ref[...]
    compliance = jnp.sum(member * pairs, axis=1, keepdims=True)
    valid = lax.broadcasted_iota(jnp.int32, (32, 1), 0) < CHANNELS
    mean = jnp.sum(compliance, axis=0, keepdims=True) * (1.0 / CHANNELS)
    away = jnp.where(valid, compliance - mean, 0.0)
    spread = jnp.sqrt(jnp.sum(away * away, axis=0, keepdims=True) * (1.0 / CHANNELS) + SPREAD_FLOOR)
    weight = (1.0 + away / spread) * (2.0 / CHANNELS)
    per_pair = jnp.sum(member * weight, axis=0, keepdims=True)
    compliance_ref[...] = column_to_row(compliance)
    total = None
    for v in range(VARIANTS):
        combined = None
        for w in range(WIDTHS):
            k = v * WIDTHS + w
            term = per_pair[:, k : k + 1] * t_ref[w, v * HALF : (v + 1) * HALF, :]
            combined = term if combined is None else combined + term
        combined = combined * s_ref[v]
        total = combined if total is None else total + combined
    out_ref[...] = total.T


def per_device(density, threshold_index, channel_width, sigma_table):
    planes, own_rows, nx = density.shape
    rows, cols = lax.axis_size("row"), lax.axis_size("col")
    ny = own_rows * rows
    cells = float(planes * ny * nx * cols)
    params = pltpu.CompilerParams(vmem_limit_bytes=24 * MIB)

    xt, y, member = pl.pallas_call(
        bands_kernel,
        out_shape=(
            jax.ShapeDtypeStruct((WIDTHS * HALF, 3 * HALF), BF16),
            jax.ShapeDtypeStruct((WIDTHS, ny, ny), BF16),
            jax.ShapeDtypeStruct((32, 128), F32),
        ),
        in_specs=[SMEM, SMEM],
        out_specs=[VMEM] * 3,
        compiler_params=params,
        cost_estimate=pl.CostEstimate(flops=10_000_000, bytes_accessed=2_500_000, transcendentals=500_000),
        name="bands",
    )(sigma_table, channel_width)

    plane = lax.all_to_all(density, "row", split_axis=0, concat_axis=0, tiled=True).reshape(ny, nx)
    up = [(i, i + 1) for i in range(cols - 1)]
    down = [(i + 1, i) for i in range(cols - 1)]
    left = lax.ppermute(plane, "col", up)
    right = lax.ppermute(plane, "col", down)

    t, s, part = pl.pallas_call(
        smooth_kernel,
        out_shape=(
            jax.ShapeDtypeStruct((WIDTHS, VARIANTS * HALF, ny), F32),
            jax.ShapeDtypeStruct((VARIANTS, HALF, ny), F32),
            jax.ShapeDtypeStruct((rows, 1, 128), F32),
        ),
        in_specs=[SMEM] + [VMEM] * 5,
        out_specs=[VMEM] * 3,
        scratch_shapes=[
            pltpu.VMEM((3 * HALF, ny), BF16),
            pltpu.VMEM((VARIANTS, HALF, ny), F32),
            pltpu.VMEM((WIDTHS, VARIANTS * HALF, ny), BF16),
            pltpu.VMEM((32, 128), F32),
        ],
        compiler_params=params,
        cost_estimate=pl.CostEstimate(flops=1_300_000_000, bytes_accessed=7_000_000, transcendentals=300_000),
        name="smooth",
    )(threshold_index, left, plane, right, xt, y)

    part = lax.all_to_all(part, "row", split_axis=0, concat_axis=0, tiled=True)
    part = pl.pallas_call(
        gather_kernel,
        out_shape=jax.ShapeDtypeStruct((cols, 1, 128), F32),
        in_specs=[VMEM],
        out_specs=VMEM,
        compiler_params=params,
        name="regroup",
    )(part)
    part = lax.all_to_all(part, "col", split_axis=0, concat_axis=0, tiled=True)

    compliance, sensitivity = pl.pallas_call(
        lambda *refs: combine_kernel(cells, *refs),
        out_shape=(
            jax.ShapeDtypeStruct((1, 128), F32),
            jax.ShapeDtypeStruct((ny, nx), F32),
        ),
        in_specs=[VMEM] * 4,
        out_specs=[VMEM] * 2,
        compiler_params=params,
        name="combine",
    )(part, member, t, s)
    sensitivity = lax.all_to_all(
        sensitivity.reshape(planes, own_rows, nx), "row", split_axis=0, concat_axis=0, tiled=True
    )
    return compliance[0, :CHANNELS], sensitivity


def solution(mesh):
    in_specs = (P(None, "row", "col"), P(), P(), P())
    out_specs = (P(), P(None, "row", "col"))
    return jax.shard_map(
        per_device, mesh=mesh, in_specs=in_specs, out_specs=out_specs, check_vma=False
    )
```

time: 866 us -> 82.8 us (0.10)
  loops' own time: 293 us -> 0 us
  other arithmetic: 219 us -> 0 us
  matrix products: 89.1 us -> 0 us
  blocking collectives: 117 us -> 52 us
  local copies, waits for them, and re-layouts: 60.6 us -> 3.12 us
  waiting for transfers between devices: 46 us -> 8.91 us
  starting transfers between devices: 32.1 us -> 10.9 us
    another operation x2 -> x0, loops' own time: 293 us -> none  [the longest x1 174 us: per_device(): smoothed, partials = lax.map(along_y, channel_ids)]
    reduce_sum x213 -> x0, other arithmetic: 217 us -> none  [the longest x60 80.9 us: width_of(): jnp.sum(jnp.where(jnp.arange(channel_width.shape[0]) == index, channel_wi...]
    psum x1 -> x0, blocking collectives: 98.4 us -> none  [per_device(): compliance = lax.psum(partials, ('row', 'col')) / cell_count]
    dot_general x61 -> x0, matrix products: 89.1 us -> none  [the longest x30 54.6 us: along_y(): jnp.einsum('zyx,yw->zwx', source, matrix, preferred_element_type=jnp.floa...]
    all_to_all x2 -> x1, waiting for transfers between devices: 45.5 us -> 8.91 us  [per_device(): lax.all_to_all(sensitivity.reshape(planes, own_rows, nx), 'row', split_ax...]
    dynamic_slice x60 -> x0, local copies, waits for them, and re-layouts: 34.9 us -> none  [per_device(): panels = lax.map(partial(smooth_x, wide), channel_ids)]
    all_to_all x1 -> x3, blocking collectives: 18.6 us -> 52 us  [the longest x1 23.1 us: per_device(): lax.all_to_all(density, 'row', split_axis=0, concat_axis=0, tiled=True)]
    dynamic_update_slice x30 -> x0, local copies, waits for them, and re-layouts: 22.7 us -> none  [per_device(): smoothed, partials = lax.map(along_y, channel_ids)]
  transfers between devices with their start and end apart: 4 -> 3, of which waited for: 2 -> 1; matrix products, arithmetic and copies ran while one was open for 16% -> 1% of each run, Pallas kernels for 0% -> 1%
where the time goes in v1:
time: 82.8 us; the launch traced here: 82.4 us
  blocking collectives  52 us (63%)
  starting transfers between devices  10.9 us (13%)
  waiting for transfers between devices  8.91 us (11%)
  Pallas kernels  6.81 us (8%)
  local copies, waits for them, and re-layouts  3.12 us (4%)
    all_to_all x1, blocking collectives, per_device(): lax.all_to_all(density, 'row', split_axis=0, concat_axis=0, tiled=True)  23.1 us
    all_to_all x1, blocking collectives, per_device(): part = lax.all_to_all(part, 'col', split_axis=0, concat_axis=0, tiled=True)  17.3 us
    all_to_all x1, blocking collectives, per_device(): part = lax.all_to_all(part, 'row', split_axis=0, concat_axis=0, tiled=True)  11.6 us
    all_to_all x1, waiting for transfers between devices, per_device(): lax.all_to_all(sensitivity.reshape(planes, own_rows, nx), 'row', split_ax...  8.91 us
    pallas_call x1, Pallas kernels, per_device(): pl.pallas_call(smooth_kernel, out_shape=(jax.ShapeDtypeStruct((WIDTHS, VA...  4.37 us
    ppermute x1, starting transfers between devices, per_device(): right = lax.ppermute(plane, 'col', down)  3.96 us
    all_to_all x1, starting transfers between devices, per_device(): lax.all_to_all(sensitivity.reshape(planes, own_rows, nx), 'row', split_ax...  3.86 us
    ppermute x1, starting transfers between devices, per_device(): left = lax.ppermute(plane, 'col', up)  3.1 us
  transfers between devices with their start and end apart: 3, of which 1 were waited for; matrix products, arithmetic and copies ran while one was open for 1% of the time, Pallas kernels for 1%

profile of v1, /device:TPU:1, one launch (start us, length us, event | category | flops | bytes accessed | tf_op | source)
XLA Modules:
  0.0 82.4 jit_solution(1105319699744913606)
XLA Ops:
  0.6 23.1 %all_to_all.20 = f32[32,8,128]{2,1,0:T(8,128)S(1)} all-to-all(f32[32,8,128]{2,1,0:T(8,128)} %param.4), channel_id=1, replica_groups=mesh['row'=32,'col'=16] {'row'}, dimensions={0} | all-to-all | bytes 262144 | tf_op jit(solution)/shard_map/all_to_all | solution.py:145
  23.7 4.0 %collective-permute-start.1 = (f32[256,128]{1,0:T(8,128)S(1)}, f32[256,128]{1,0:T(8,128)S(1)}, u32[]{:S(2)}, u32[]{:S(2)}) collective-permute-start(f32[256,128]{1,0:T(8,128)S(1)} %bitcast.4), channel_id=1, source_target_pairs={{1,0},{2,1},{3,2},{4,3},{5,4},{6,5},{7,6},{8,7},{9,8},{10,9},{11,1... | collective-permute-start | bytes 393224 | tf_op jit(solution)/shard_map/ppermute | solution.py:149
  27.7 3.1 %collective-permute-start = (f32[256,128]{1,0:T(8,128)S(1)}, f32[256,128]{1,0:T(8,128)S(1)}, u32[]{:S(2)}, u32[]{:S(2)}) collective-permute-start(f32[256,128]{1,0:T(8,128)S(1)} %bitcast.5), channel_id=1, source_target_pairs={{0,1},{1,2},{2,3},{3,4},{4,5},{5,6},{6,7},{7,8},{8,9},{9,10},{10,1... | collective-permute-start | bytes 393224 | tf_op jit(solution)/shard_map/ppermute | solution.py:148
  30.8 0.0 copy-start
  30.8 0.6 copy-done
  31.4 0.0 copy-start.1
  31.4 0.7 copy-done.1
  32.1 1.2 %bands.1 = (bf16[1280,384]{1,0:T(8,128)(2,1)S(1)}, bf16[10,256,256]{2,1,0:T(8,128)(2,1)S(1)}, f32[32,128]{1,0:T(8,128)S(1)}) custom-call(f32[10]{0:T(128)S(1)} %copy-done, s32[30]{0:T(128)S(1)} %copy-done.1), custom_call_target="tpu_custom_call" | custom-call | flops 10000000 | bytes 2500000 | tf_op jit(solution)/shard_map/bands/pallas_call | solution.py:131
  33.3 0.0 collective-permute-done.1.right_ref
  33.3 0.0 collective-permute-done.left_ref
  33.3 0.0 copy-start.2
  33.3 0.6 copy-done.2
  33.9 4.4 %smooth.1 = (f32[10,384,256]{2,1,0:T(8,128)S(1)}, f32[3,128,256]{2,1,0:T(8,128)S(1)}, f32[32,1,128]{2,1,0:T(1,128)S(1)}) custom-call(s32[3]{0:T(128)S(1)} %copy-done.2, f32[256,128]{1,0:T(8,128)S(1)} %collective-permute-done.left_ref, f32[256,128]{1,0:T(8,128)S(1)} %bitcast.6, f32[256,128]{1,0:T(8,128)S(1)} %collective-permute-done.1.right_ref, ...), custom_call_target="tpu_custom_call" | custom-call | flops 1300000000 | bytes 7000000 | tf_op jit(solution)/shard_map/smooth/pallas_call | solution.py:151
  38.3 11.6 %all_to_all.21.in_ref = f32[32,1,128]{2,1,0:T(1,128)S(1)} all-to-all(f32[32,1,128]{2,1,0:T(1,128)S(1)} %get-tuple-element.12), channel_id=1, replica_groups=mesh['row'=32,'col'=16] {'row'}, dimensions={0} | all-to-all | bytes 32768 | tf_op jit(solution)/shard_map/all_to_all | solution.py:171
  50.0 17.3 %all_to_all.22.refs_0_ = f32[16,1,128]{2,1,0:T(1,128)S(1)} all-to-all(f32[16,1,128]{2,1,0:T(1,128)S(1)} %regroup.1), channel_id=1, replica_groups=mesh['row'=32,'col'=16] {'col'}, dimensions={0} | all-to-all | bytes 16384 | tf_op jit(solution)/shard_map/all_to_all | solution.py:180
  67.2 1.2 %combine.1 = (f32[1,128]{1,0:T(1,128)S(1)}, f32[256,128]{1,0:T(8,128)}) custom-call(f32[16,1,128]{2,1,0:T(1,128)S(1)} %all_to_all.22.refs_0_, f32[32,128]{1,0:T(8,128)S(1)} %get-tuple-element.13.refs_1_, f32[10,384,256]{2,1,0:T(8,128)S(1)} %get-tuple-element.14.refs_2_, f32[3,128,256]{2,1,0:T(8,128)S(1)} %get-tuple-element.15.refs_3_), custom_call_target="tpu_custom_call" | custom-call | tf_op jit(solution)/shard_map/combine/pallas_call | solution.py:182
  68.5 3.9 %all-to-all-start.3 = ((f32[32,8,128]{2,1,0:T(8,128)}), f32[32,8,128]{2,1,0:T(8,128)S(1)}, u32[]{:S(2)}, u32[]{:S(2)}) async-start(f32[32,8,128]{2,1,0:T(8,128)} %bitcast.2), calls=%async_computation.3 | async-start | bytes 262144 | tf_op jit(solution)/shard_map/all_to_all | solution.py:193
  72.3 0.5 slice_bitcast_fusion
  72.9 8.9 %all-to-all-done.3 = f32[32,8,128]{2,1,0:T(8,128)S(1)} async-done(((f32[32,8,128]{2,1,0:T(8,128)}), f32[32,8,128]{2,1,0:T(8,128)S(1)}, u32[]{:S(2)}, u32[]{:S(2)}) %all-to-all-start.3) | async-done | bytes 131104 | tf_op jit(solution)/shard_map/all_to_all | solution.py:193
  81.8 0.7 copy.7
  (1 shorter events, 0.0 us)
Async XLA Ops:
  23.7 9.6 %collective-permute-start.1 = (f32[256,128]{1,0:T(8,128)S(1)}, f32[256,128]{1,0:T(8,128)S(1)}, u32[]{:S(2)}, u32[]{:S(2)}) collective-permute-start(f32[256,128]{1,0:T(8,128)S(1)} %bitcast.4), channel_id=1, source_target_pairs={{1,0},{2,1},{3,2},{4,3},{5,4},{6,5},{7,6},{8,7},{9,8},{10,9},{11,1... | collective-permute-start | bytes 393224 | tf_op jit(solution)/shard_map/ppermute | solution.py:149
  27.7 5.6 %collective-permute-start = (f32[256,128]{1,0:T(8,128)S(1)}, f32[256,128]{1,0:T(8,128)S(1)}, u32[]{:S(2)}, u32[]{:S(2)}) collective-permute-start(f32[256,128]{1,0:T(8,128)S(1)} %bitcast.5), channel_id=1, source_target_pairs={{0,1},{1,2},{2,3},{3,4},{4,5},{5,6},{6,7},{7,8},{8,9},{9,10},{10,1... | collective-permute-start | bytes 393224 | tf_op jit(solution)/shard_map/ppermute | solution.py:148
  30.8 0.7 copy-start
  31.4 0.7 copy-start.1
  33.3 0.7 copy-start.2
  68.5 13.3 %all-to-all-start.3 = ((f32[32,8,128]{2,1,0:T(8,128)}), f32[32,8,128]{2,1,0:T(8,128)S(1)}, u32[]{:S(2)}, u32[]{:S(2)}) async-start(f32[32,8,128]{2,1,0:T(8,128)} %bitcast.2), calls=%async_computation.3 | async-start | bytes 262144 | tf_op jit(solution)/shard_map/all_to_all | solution.py:193

commit v2 on v1

v2 whole, which is shorter than its diff:
```python
import jax
import jax.numpy as jnp
from jax import lax
from jax.experimental import pallas as pl
from jax.experimental.pallas import tpu as pltpu
from jax.sharding import PartitionSpec as P

VARIANTS = 3
WIDTHS = 10
CHANNELS = 30
HALF = 128
SHARPNESS = 8.0
SPREAD_FLOOR = 0.0001

F32 = jnp.float32
BF16 = jnp.bfloat16
VMEM = pl.BlockSpec(memory_space=pltpu.VMEM)
SMEM = pl.BlockSpec(memory_space=pltpu.SMEM)
MIB = 1024 * 1024


def bands_kernel(sigma_ref, width_ref, index_ref, xt_ref, member_ref, level_ref):
    row = lax.broadcasted_iota(jnp.int32, (HALF, HALF), 0)
    col = lax.broadcasted_iota(jnp.int32, (HALF, HALF), 1)
    gap = col - row
    gap_f = gap.astype(F32)
    squares = ((gap_f - HALF) ** 2, gap_f * gap_f, (gap_f + HALF) ** 2)
    masks = (gap >= 0, None, gap <= 0)
    taps = lax.broadcasted_iota(jnp.int32, (1, HALF), 1).astype(F32) + 1.0
    for w in range(WIDTHS):
        sigma = jnp.full((1, HALF), sigma_ref[w], F32)
        scale = -1.0 / (2.0 * sigma * sigma)
        total = 1.0 + 2.0 * jnp.sum(jnp.exp(taps * taps * scale), axis=1, keepdims=True)
        inverse = 1.0 / total
        blocks = []
        for square, mask in zip(squares, masks):
            value = jnp.exp(square * scale) * inverse
            if mask is not None:
                value = jnp.where(mask, value, 0.0)
            blocks.append(value.astype(BF16))
        before, middle, after = blocks
        rows = slice(w * HALF, (w + 1) * HALF)
        xt_ref[rows, 0:HALF] = before
        xt_ref[rows, HALF : 2 * HALF] = middle
        xt_ref[rows, 2 * HALF : 3 * HALF] = after
    lane = lax.broadcasted_iota(jnp.int32, (1, 128), 1)
    for c in range(CHANNELS):
        pair = (c // WIDTHS) * WIDTHS + width_ref[c]
        member_ref[c : c + 1, :] = (lane == pair).astype(F32)
    member_ref[CHANNELS:32, :] = jnp.zeros((32 - CHANNELS, 128), F32)
    for v in range(VARIANTS):
        level = jnp.full((1, 128), index_ref[v].astype(F32) * (1.0 / 16.0), F32)
        low = jnp.tanh(SHARPNESS * level)
        high = jnp.tanh(SHARPNESS * (1.0 - level))
        level_ref[v : v + 1, :] = level
        level_ref[8 + v : 9 + v, :] = low
        level_ref[16 + v : 17 + v, :] = 1.0 / (low + high)


def column_to_row(column):
    rows = column.shape[0]
    at = lax.broadcasted_iota(jnp.int32, (rows, 128), 0) == lax.broadcasted_iota(jnp.int32, (rows, 128), 1)
    return jnp.sum(jnp.where(at, jnp.broadcast_to(column, (rows, 128)), 0.0), axis=0, keepdims=True)


def constants(level_ref, v, width):
    rows = [level_ref[8 * i + v : 8 * i + v + 1, :] for i in range(3)]
    return [jnp.concatenate([row] * (width // 128), axis=1) for row in rows]


def project(side, level, low, inverse):
    inner = jnp.tanh(SHARPNESS * (side - level))
    return ((low + inner) * inverse).astype(BF16), inner


def square_band(xt_ref, w):
    rows = pl.ds(w * HALF, HALF)
    return jnp.concatenate([xt_ref[rows, HALF : 3 * HALF], xt_ref[rows, 0 : 2 * HALF]], axis=0)


def own_kernel(own_ref, xt_ref, level_ref, b_ref, rows_ref, p_ref, a_ref):
    ny = own_ref.shape[0]
    own = own_ref[...].T
    for v in range(VARIANTS):
        level, low, inverse = constants(level_ref, v, ny)
        value, _ = project(own, level, low, inverse)
        p_ref[v * HALF : (v + 1) * HALF, :] = value
        along = jnp.dot(xt_ref[:, HALF : 2 * HALF], value, preferred_element_type=F32)
        a_ref[:, v * HALF : (v + 1) * HALF, :] = along.reshape(WIDTHS, HALF, ny)
    rows_ref[...] = jnp.zeros_like(rows_ref)

    def per_width(w, carry):
        b = jnp.dot(p_ref[...], square_band(xt_ref, w), preferred_element_type=F32)
        b_ref[w] = b
        product = a_ref[w] * b
        for v in range(VARIANTS):
            line = jnp.sum(product[v * HALF : (v + 1) * HALF, :], axis=0, keepdims=True)
            rows_ref[pl.ds(v * WIDTHS + w, 1), :] = line[:, 0:128] + line[:, 128:256]
        return carry

    lax.fori_loop(0, WIDTHS, per_width, 0)


def cross_kernel(right_ref, xt_ref, level_ref, b_ref, own_rows_ref, part_ref, rows_ref):
    ny = right_ref.shape[0]
    right = right_ref[...].T
    rows_ref[...] = own_rows_ref[...]
    for v in range(VARIANTS):
        level, low, inverse = constants(level_ref, v, ny)
        value, _ = project(right, level, low, inverse)
        along = jnp.dot(xt_ref[:, 2 * HALF : 3 * HALF], value, preferred_element_type=F32)
        for w in range(WIDTHS):
            product = along[w * HALF : (w + 1) * HALF, :] * b_ref[w, v * HALF : (v + 1) * HALF, :]
            line = jnp.sum(product, axis=0, keepdims=True)
            k = v * WIDTHS + w
            rows_ref[k : k + 1, :] += 2.0 * (line[:, 0:128] + line[:, 128:256])
    sums = column_to_row(jnp.sum(rows_ref[...], axis=1, keepdims=True))
    part_ref[...] = jnp.broadcast_to(sums.reshape(1, 1, 128), part_ref.shape)


def along_kernel(left_ref, own_ref, right_ref, xt_ref, level_ref, a_ref, p_ref):
    ny = left_ref.shape[0]
    left, own, right = left_ref[...].T, own_ref[...].T, right_ref[...].T
    for v in range(VARIANTS):
        level, low, inverse = constants(level_ref, v, ny)
        p_ref[0:HALF, :] = project(left, level, low, inverse)[0]
        p_ref[HALF : 2 * HALF, :] = project(own, level, low, inverse)[0]
        p_ref[2 * HALF : 3 * HALF, :] = project(right, level, low, inverse)[0]
        along = jnp.dot(xt_ref[...], p_ref[...], preferred_element_type=F32).astype(BF16)
        a_ref[:, v * HALF : (v + 1) * HALF, :] = along.reshape(WIDTHS, HALF, ny)


def gather_kernel(in_ref, out_ref):
    total = jnp.sum(in_ref[...], axis=0, keepdims=True)
    out_ref[...] = jnp.broadcast_to(total, out_ref.shape)


def combine_kernel(cells, sums_ref, member_ref, a_ref, own_ref, xt_ref, level_ref, compliance_ref, out_ref, total_ref):
    pairs = jnp.sum(sums_ref[...], axis=0) * (1.0 / cells)
    member = member_ref[...]
    compliance = jnp.sum(member * pairs, axis=1, keepdims=True)
    valid = lax.broadcasted_iota(jnp.int32, (32, 1), 0) < CHANNELS
    mean = jnp.sum(compliance, axis=0, keepdims=True) * (1.0 / CHANNELS)
    away = jnp.where(valid, compliance - mean, 0.0)
    spread = jnp.sqrt(jnp.sum(away * away, axis=0, keepdims=True) * (1.0 / CHANNELS) + SPREAD_FLOOR)
    weight = (1.0 + away / spread) * (2.0 / CHANNELS)
    per_pair = jnp.sum(member * weight, axis=0, keepdims=True)
    compliance_ref[...] = column_to_row(compliance)[0, :CHANNELS]
    for w in range(WIDTHS):
        field = jnp.dot(a_ref[w], square_band(xt_ref, w), preferred_element_type=F32)
        for v in range(VARIANTS):
            k = v * WIDTHS + w
            term = per_pair[:, k : k + 1] * field[v * HALF : (v + 1) * HALF, :]
            total_ref[v] = term if w == 0 else total_ref[v] + term
    own = own_ref[...].T
    total = None
    for v in range(VARIANTS):
        level, low, inverse = constants(level_ref, v, own.shape[1])
        inner = jnp.tanh(SHARPNESS * (own - level))
        term = total_ref[v] * (SHARPNESS * (1.0 - inner * inner) * inverse)
        total = term if total is None else total + term
    out_ref[...] = total.T


def call(kernel, name, out, inputs, scratch=(), specs=None, flops=0, moved=0, special=0):
    return pl.pallas_call(
        kernel,
        out_shape=tuple(jax.ShapeDtypeStruct(shape, dtype) for shape, dtype in out),
        in_specs=specs or [VMEM] * len(inputs),
        out_specs=(VMEM,) * len(out),
        scratch_shapes=list(scratch),
        compiler_params=pltpu.CompilerParams(vmem_limit_bytes=24 * MIB),
        cost_estimate=pl.CostEstimate(flops=flops, bytes_accessed=moved, transcendentals=special),
        name=name,
    )(*inputs)


def per_device(density, threshold_index, channel_width, sigma_table):
    planes, own_rows, nx = density.shape
    rows, cols = lax.axis_size("row"), lax.axis_size("col")
    ny = own_rows * rows
    cells = float(planes * ny * nx * cols)
    tall = VARIANTS * HALF

    xt, member, levels = call(
        bands_kernel,
        "bands",
        (((WIDTHS * HALF, 3 * HALF), BF16), ((32, 128), F32), ((24, 128), F32)),
        (sigma_table, channel_width, threshold_index),
        specs=[SMEM] * 3,
        flops=10_000_000,
        moved=2_500_000,
        special=500_000,
    )
    plane = lax.all_to_all(density, "row", split_axis=0, concat_axis=0, tiled=True).reshape(ny, nx)
    plane, xt, member, levels = lax.optimization_barrier((plane, xt, member, levels))
    right = lax.ppermute(plane, "col", [(i + 1, i) for i in range(cols - 1)])

    b, own_rows_sum = call(
        own_kernel,
        "own",
        (((WIDTHS, tall, ny), F32), ((32, 128), F32)),
        (plane, xt, levels),
        scratch=(pltpu.VMEM((tall, ny), BF16), pltpu.VMEM((WIDTHS, tall, ny), F32)),
        flops=750_000_000,
        moved=7_000_000,
        special=100_000,
    )
    (part,) = call(
        cross_kernel,
        "cross",
        (((rows, 1, 128), F32),),
        (right, xt, levels, b, own_rows_sum),
        scratch=(pltpu.VMEM((32, 128), F32),),
        flops=250_000_000,
        moved=5_000_000,
        special=100_000,
    )
    later, part = lax.optimization_barrier((plane, part))
    left = lax.ppermute(later, "col", [(i, i + 1) for i in range(cols - 1)])
    part = lax.all_to_all(part, "row", split_axis=0, concat_axis=0, tiled=True)
    (part,) = call(gather_kernel, "regroup", (((cols, 1, 128), F32),), (part,))
    part = lax.all_to_all(part, "col", split_axis=0, concat_axis=0, tiled=True)

    (a,) = call(
        along_kernel,
        "along",
        (((WIDTHS, tall, ny), BF16),),
        (left, plane, right, xt, levels),
        scratch=(pltpu.VMEM((3 * HALF, ny), BF16),),
        flops=800_000_000,
        moved=4_000_000,
        special=300_000,
    )
    compliance, sensitivity = call(
        lambda *refs: combine_kernel(cells, *refs),
        "combine",
        (((CHANNELS,), F32), ((ny, nx), F32)),
        (part, member, a, plane, xt, levels),
        scratch=(pltpu.VMEM((VARIANTS, HALF, ny), F32),),
        flops=500_000_000,
        moved=5_000_000,
    )
    sensitivity = lax.all_to_all(
        sensitivity.reshape(planes, own_rows, nx), "row", split_axis=0, concat_axis=0, tiled=True
    )
    return compliance, sensitivity


def solution(mesh):
    in_specs = (P(None, "row", "col"), P(), P(), P())
    out_specs = (P(), P(None, "row", "col"))
    return jax.shard_map(
        per_device, mesh=mesh, in_specs=in_specs, out_specs=out_specs, check_vma=False
    )
```

time: 82.8 us -> 76.5 us (0.924)
  blocking collectives: 52 us -> 24 us
  starting transfers between devices: 10.9 us -> 27.9 us
  waiting for transfers between devices: 8.91 us -> 12.5 us
  Pallas kernels: 6.81 us -> 8.3 us
    all_to_all x2 -> x1, blocking collectives: 40.3 us -> 12.4 us  [per_device(): lax.all_to_all(sensitivity.reshape(planes, own_rows, nx), 'row', split_ax...]
    all_to_all x1 -> x2, starting transfers between devices: 3.86 us -> 21.6 us  [the longest x1 13.7 us: per_device(): lax.all_to_all(density, 'row', split_axis=0, concat_axis=0, tiled=True)]
    all_to_all x1 -> x2, waiting for transfers between devices: 8.91 us -> 11.8 us  [the longest x1 6.29 us: per_device(): lax.all_to_all(density, 'row', split_axis=0, concat_axis=0, tiled=True)]
    pallas_call x4 -> x6, Pallas kernels: 6.81 us -> 8.3 us  [call(): pl.pallas_call(kernel, out_shape=tuple((jax.ShapeDtypeStruct(shape, dtype...]
  transfers between devices with their start and end apart: 3 -> 4, of which waited for: 1 -> 3; matrix products, arithmetic and copies ran while one was open for 1% -> 0% of each run, Pallas kernels for 1% -> 8%
where the time goes in v2:
time: 76.5 us; the launch traced here: 76.1 us
  starting transfers between devices  27.9 us (36%)
  blocking collectives  24 us (31%)
  waiting for transfers between devices  12.5 us (16%)
  Pallas kernels  8.3 us (11%)
  local copies, waits for them, and re-layouts  2.62 us (3%)
    all_to_all x1, starting transfers between devices, per_device(): lax.all_to_all(density, 'row', split_axis=0, concat_axis=0, tiled=True)  13.7 us
    all_to_all x1, blocking collectives, per_device(): lax.all_to_all(sensitivity.reshape(planes, own_rows, nx), 'row', split_ax...  12.4 us
    all_to_all x1, blocking collectives, per_device(): part = lax.all_to_all(part, 'row', split_axis=0, concat_axis=0, tiled=True)  11.6 us
    pallas_call x6, Pallas kernels, call(): pl.pallas_call(kernel, out_shape=tuple((jax.ShapeDtypeStruct(shape, dtype...  8.3 us
    all_to_all x1, starting transfers between devices, per_device(): part = lax.all_to_all(part, 'col', split_axis=0, concat_axis=0, tiled=True)  7.85 us
    all_to_all x1, waiting for transfers between devices, per_device(): lax.all_to_all(density, 'row', split_axis=0, concat_axis=0, tiled=True)  6.29 us
    all_to_all x1, waiting for transfers between devices, per_device(): part = lax.all_to_all(part, 'col', split_axis=0, concat_axis=0, tiled=True)  5.54 us
    ppermute x1, starting transfers between devices, per_device(): right = lax.ppermute(plane, 'col', [(i + 1, i) for i in range(cols - 1)])  3.96 us
  transfers between devices with their start and end apart: 4, of which 3 were waited for; matrix products, arithmetic and copies ran while one was open for 0% of the time, Pallas kernels for 8%

profile of v2, /device:TPU:1, one launch (start us, length us, event | category | flops | bytes accessed | tf_op | source)
XLA Modules:
  0.0 76.1 jit_solution(9721555708535021681)
XLA Ops:
  0.6 13.7 %all-to-all-start = ((f32[32,8,128]{2,1,0:T(8,128)}), f32[32,8,128]{2,1,0:T(8,128)S(1)}, u32[]{:S(2)}, u32[]{:S(2)}) async-start(f32[32,8,128]{2,1,0:T(8,128)} %param.4), calls=%async_computation | async-start | bytes 262144 | tf_op jit(solution)/shard_map/all_to_all | solution.py:195
  14.4 0.0 copy-start
  14.4 0.6 copy-done
  15.0 0.0 copy-start.1
  15.0 0.7 copy-done.1
  15.7 0.0 copy-start.2
  15.7 0.7 copy-done.2
  16.3 1.1 %bands.1 = (bf16[1280,384]{1,0:T(8,128)(2,1)S(1)}, f32[32,128]{1,0:T(8,128)S(1)}, f32[24,128]{1,0:T(8,128)S(1)}) custom-call(f32[10]{0:T(128)S(1)} %copy-done, s32[30]{0:T(128)S(1)} %copy-done.1, s32[3]{0:T(128)S(1)} %copy-done.2), custom_call_target="tpu_custom_call" | custom-call | flops 10000000 | bytes 2500000 | tf_op jit(solution)/shard_map/bands/pallas_call | solution.py:166
  17.4 6.3 %all-to-all-done = f32[32,8,128]{2,1,0:T(8,128)S(1)} async-done(((f32[32,8,128]{2,1,0:T(8,128)}), f32[32,8,128]{2,1,0:T(8,128)S(1)}, u32[]{:S(2)}, u32[]{:S(2)}) %all-to-all-start) | async-done | bytes 131104 | tf_op jit(solution)/shard_map/all_to_all | solution.py:195
  23.7 4.0 %collective-permute-start = (f32[256,128]{1,0:T(8,128)S(1)}, f32[256,128]{1,0:T(8,128)S(1)}, u32[]{:S(2)}, u32[]{:S(2)}) collective-permute-start(f32[256,128]{1,0:T(8,128)S(1)} %bitcast.2), channel_id=1, source_target_pairs={{1,0},{2,1},{3,2},{4,3},{5,4},{6,5},{7,6},{8,7},{9,8},{10,9},{11,1... | collective-permute-start | bytes 393224 | tf_op jit(solution)/shard_map/ppermute | solution.py:197
  27.7 3.1 %own.1 = (f32[10,384,256]{2,1,0:T(8,128)S(1)}, f32[32,128]{1,0:T(8,128)S(1)}) custom-call(f32[256,128]{1,0:T(8,128)S(1)} %bitcast.3, bf16[1280,384]{1,0:T(8,128)(2,1)S(1)} %get-tuple-element.19.xt_ref.refs_4_, f32[24,128]{1,0:T(8,128)S(1)} %get-tuple-element.20.level_ref.refs_5_), custom_call_target="tpu_custom_call" | custom-call | flops 750000000 | bytes 7000000 | tf_op jit(solution)/shard_map/own/pallas_call | solution.py:166
  30.8 0.7 collective-permute-done.right_ref
  31.5 0.9 %cross.1 = f32[32,1,128]{2,1,0:T(1,128)S(1)} custom-call(f32[256,128]{1,0:T(8,128)S(1)} %collective-permute-done.right_ref, bf16[1280,384]{1,0:T(8,128)(2,1)S(1)} %get-tuple-element.19.xt_ref.refs_4_, f32[24,128]{1,0:T(8,128)S(1)} %get-tuple-element.20.level_ref.refs_5_, f32[10,384,256]{2,1,0:T(8,128)S(1)} %get-tuple-element.21.b_ref, ...), custom_call_target="tpu_custom_call" | custom-call | flops 250000000 | bytes 5000000 | tf_op jit(solution)/shard_map/cross/pallas_call | solution.py:166
  32.4 2.4 %collective-permute-start.1 = (f32[256,128]{1,0:T(8,128)S(1)}, f32[256,128]{1,0:T(8,128)S(1)}, u32[]{:S(2)}, u32[]{:S(2)}) collective-permute-start(f32[256,128]{1,0:T(8,128)S(1)} %bitcast.4), channel_id=1, source_target_pairs={{0,1},{1,2},{2,3},{3,4},{4,5},{5,6},{6,7},{7,8},{8,9},{9,10},{10,1... | collective-permute-start | bytes 393224 | tf_op jit(solution)/shard_map/ppermute | solution.py:220
  34.8 11.6 %all_to_all.20.in_ref = f32[32,1,128]{2,1,0:T(1,128)S(1)} all-to-all(f32[32,1,128]{2,1,0:T(1,128)S(1)} %cross.1), channel_id=1, replica_groups=mesh['row'=32,'col'=16] {'row'}, dimensions={0} | all-to-all | bytes 32768 | tf_op jit(solution)/shard_map/all_to_all | solution.py:221
  46.4 0.6 regroup.1
  47.1 7.9 %all-to-all-start.2 = ((f32[16,1,128]{2,1,0:T(1,128)}), f32[16,1,128]{2,1,0:T(1,128)S(1)}, u32[]{:S(2)}, u32[]{:S(2)}) async-start(f32[16,1,128]{2,1,0:T(1,128)} %regroup.1), calls=%async_computation.2 | async-start | bytes 16384 | tf_op jit(solution)/shard_map/all_to_all | solution.py:223
  54.9 0.0 collective-permute-done.1.left_ref
  54.9 1.4 %along.1.refs_2_ = bf16[10,384,256]{2,1,0:T(8,128)(2,1)S(1)} custom-call(f32[256,128]{1,0:T(8,128)S(1)} %collective-permute-done.1.left_ref, f32[256,128]{1,0:T(8,128)S(1)} %bitcast.5, f32[256,128]{1,0:T(8,128)S(1)} %collective-permute-done.right_ref, bf16[1280,384]{1,0:T(8,128)(2,1)S(1)} %get-tuple-element.19.xt_ref.refs_4_, ...), custom_call_target="tpu_custom_call" | custom-call | flops 800000000 | bytes 4000000 | tf_op jit(solution)/shard_map/along/pallas_call | solution.py:166
  56.3 5.5 %all-to-all-done.2.refs_0_ = f32[16,1,128]{2,1,0:T(1,128)S(1)} async-done(((f32[16,1,128]{2,1,0:T(1,128)}), f32[16,1,128]{2,1,0:T(1,128)S(1)}, u32[]{:S(2)}, u32[]{:S(2)}) %all-to-all-start.2) | async-done | bytes 8224 | tf_op jit(solution)/shard_map/all_to_all | solution.py:223
  61.8 1.2 %combine.1 = (f32[30]{0:T(128)}, f32[256,128]{1,0:T(8,128)S(1)}) custom-call(f32[16,1,128]{2,1,0:T(1,128)S(1)} %all-to-all-done.2.refs_0_, f32[32,128]{1,0:T(8,128)S(1)} %get-tuple-element.24.refs_1_, bf16[10,384,256]{2,1,0:T(8,128)(2,1)S(1)} %along.1.refs_2_, f32[256,128]{1,0:T(8,128)S(1)} %bitcast.6, ...), custom_call_target="tpu_custom_call" | custom-call | flops 500000000 | bytes 5000000 | tf_op jit(solution)/shard_map/combine/pallas_call | solution.py:166
  63.1 12.4 %all_to_all.21 = f32[32,8,128]{2,1,0:T(8,128)S(1)} all-to-all(f32[32,8,128]{2,1,0:T(8,128)S(1)} %bitcast.7), channel_id=1, replica_groups=mesh['row'=32,'col'=16] {'row'}, dimensions={0} | all-to-all | bytes 262144 | tf_op jit(solution)/shard_map/all_to_all | solution.py:244
  75.5 0.7 copy.7
Async XLA Ops:
  0.6 23.1 %all-to-all-start = ((f32[32,8,128]{2,1,0:T(8,128)}), f32[32,8,128]{2,1,0:T(8,128)S(1)}, u32[]{:S(2)}, u32[]{:S(2)}) async-start(f32[32,8,128]{2,1,0:T(8,128)} %param.4), calls=%async_computation | async-start | bytes 262144 | tf_op jit(solution)/shard_map/all_to_all | solution.py:195
  14.4 0.7 copy-start
  15.0 0.7 copy-start.1
  15.7 0.7 copy-start.2
  23.7 7.8 %collective-permute-start = (f32[256,128]{1,0:T(8,128)S(1)}, f32[256,128]{1,0:T(8,128)S(1)}, u32[]{:S(2)}, u32[]{:S(2)}) collective-permute-start(f32[256,128]{1,0:T(8,128)S(1)} %bitcast.2), channel_id=1, source_target_pairs={{1,0},{2,1},{3,2},{4,3},{5,4},{6,5},{7,6},{8,7},{9,8},{10,9},{11,1... | collective-permute-start | bytes 393224 | tf_op jit(solution)/shard_map/ppermute | solution.py:197
  32.4 22.5 %collective-permute-start.1 = (f32[256,128]{1,0:T(8,128)S(1)}, f32[256,128]{1,0:T(8,128)S(1)}, u32[]{:S(2)}, u32[]{:S(2)}) collective-permute-start(f32[256,128]{1,0:T(8,128)S(1)} %bitcast.4), channel_id=1, source_target_pairs={{0,1},{1,2},{2,3},{3,4},{4,5},{5,6},{6,7},{7,8},{8,9},{9,10},{10,1... | collective-permute-start | bytes 393224 | tf_op jit(solution)/shard_map/ppermute | solution.py:220
  47.1 14.8 %all-to-all-start.2 = ((f32[16,1,128]{2,1,0:T(1,128)}), f32[16,1,128]{2,1,0:T(1,128)S(1)}, u32[]{:S(2)}, u32[]{:S(2)}) async-start(f32[16,1,128]{2,1,0:T(1,128)} %regroup.1), calls=%async_computation.2 | async-start | bytes 16384 | tf_op jit(solution)/shard_map/all_to_all | solution.py:223

commit v3 on v2

--- a/solution.py
+++ b/solution.py
@@ -85,20 +85,18 @@
         level, low, inverse = constants(level_ref, v, ny)
         value, _ = project(own, level, low, inverse)
         p_ref[v * HALF : (v + 1) * HALF, :] = value
-        along = jnp.dot(xt_ref[:, HALF : 2 * HALF], value, preferred_element_type=F32)
+    rows_ref[...] = jnp.zeros_like(rows_ref)
+    for v in range(VARIANTS):
+        part = p_ref[v * HALF : (v + 1) * HALF, :]
+        along = jnp.dot(xt_ref[:, HALF : 2 * HALF], part, preferred_element_type=F32)
         a_ref[:, v * HALF : (v + 1) * HALF, :] = along.reshape(WIDTHS, HALF, ny)
-    rows_ref[...] = jnp.zeros_like(rows_ref)
-
-    def per_width(w, carry):
+    for w in range(WIDTHS):
         b = jnp.dot(p_ref[...], square_band(xt_ref, w), preferred_element_type=F32)
         b_ref[w] = b
         product = a_ref[w] * b
         for v in range(VARIANTS):
             line = jnp.sum(product[v * HALF : (v + 1) * HALF, :], axis=0, keepdims=True)
-            rows_ref[pl.ds(v * WIDTHS + w, 1), :] = line[:, 0:128] + line[:, 128:256]
-        return carry
-
-    lax.fori_loop(0, WIDTHS, per_width, 0)
+            rows_ref[v * WIDTHS + w : v * WIDTHS + w + 1, :] = line[:, 0:128] + line[:, 128:256]
 
 
 def cross_kernel(right_ref, xt_ref, level_ref, b_ref, own_rows_ref, part_ref, rows_ref):
@@ -196,6 +194,7 @@
     plane, xt, member, levels = lax.optimization_barrier((plane, xt, member, levels))
     right = lax.ppermute(plane, "col", [(i + 1, i) for i in range(cols - 1)])
 
+    left = lax.ppermute(plane, "col", [(i, i + 1) for i in range(cols - 1)])
     b, own_rows_sum = call(
         own_kernel,
         "own",
@@ -216,8 +215,6 @@
         moved=5_000_000,
         special=100_000,
     )
-    later, part = lax.optimization_barrier((plane, part))
-    left = lax.ppermute(later, "col", [(i, i + 1) for i in range(cols - 1)])
     part = lax.all_to_all(part, "row", split_axis=0, concat_axis=0, tiled=True)
     (part,) = call(gather_kernel, "regroup", (((cols, 1, 128), F32),), (part,))
     part = lax.all_to_all(part, "col", split_axis=0, concat_axis=0, tiled=True)

time: 76.5 us -> 74.7 us (0.976)
  Pallas kernels: 8.3 us -> 6.51 us
    pallas_call x6, Pallas kernels: 8.3 us -> 6.51 us  [call(): pl.pallas_call(kernel, out_shape=tuple((jax.ShapeDtypeStruct(shape, dtype...]
  transfers between devices with their start and end apart: 4 -> 4, of which waited for: 3 -> 2; matrix products, arithmetic and copies ran while one was open for 0% -> 0% of each run, Pallas kernels for 8% -> 7%
where the time goes in v3:
time: 74.7 us; the launch traced here: 74.3 us
  starting transfers between devices  28.6 us (38%)
  blocking collectives  24 us (32%)
  waiting for transfers between devices  11.8 us (16%)
  Pallas kernels  6.51 us (9%)
  local copies, waits for them, and re-layouts  2.62 us (4%)
    all_to_all x1, starting transfers between devices, per_device(): lax.all_to_all(density, 'row', split_axis=0, concat_axis=0, tiled=True)  13.7 us
    all_to_all x1, blocking collectives, per_device(): lax.all_to_all(sensitivity.reshape(planes, own_rows, nx), 'row', split_ax...  12.4 us
    all_to_all x1, blocking collectives, per_device(): part = lax.all_to_all(part, 'row', split_axis=0, concat_axis=0, tiled=True)  11.6 us
    all_to_all x1, starting transfers between devices, per_device(): part = lax.all_to_all(part, 'col', split_axis=0, concat_axis=0, tiled=True)  7.86 us
    pallas_call x6, Pallas kernels, call(): pl.pallas_call(kernel, out_shape=tuple((jax.ShapeDtypeStruct(shape, dtype...  6.51 us
    all_to_all x1, waiting for transfers between devices, per_device(): lax.all_to_all(density, 'row', split_axis=0, concat_axis=0, tiled=True)  6.29 us
    all_to_all x1, waiting for transfers between devices, per_device(): part = lax.all_to_all(part, 'col', split_axis=0, concat_axis=0, tiled=True)  5.55 us
    ppermute x1, starting transfers between devices, per_device(): right = lax.ppermute(plane, 'col', [(i + 1, i) for i in range(cols - 1)])  3.96 us
  transfers between devices with their start and end apart: 4, of which 2 were waited for; matrix products, arithmetic and copies ran while one was open for 0% of the time, Pallas kernels for 7%

profile of v3, /device:TPU:1, one launch (start us, length us, event | category | flops | bytes accessed | tf_op | source)
XLA Modules:
  0.0 74.3 jit_solution(2917177555548813487)
XLA Ops:
  0.6 13.7 %all-to-all-start = ((f32[32,8,128]{2,1,0:T(8,128)}), f32[32,8,128]{2,1,0:T(8,128)S(1)}, u32[]{:S(2)}, u32[]{:S(2)}) async-start(f32[32,8,128]{2,1,0:T(8,128)} %param.4), calls=%async_computation | async-start | bytes 262144 | tf_op jit(solution)/shard_map/all_to_all | solution.py:193
  14.4 0.0 copy-start
  14.4 0.6 copy-done
  15.0 0.0 copy-start.1
  15.0 0.7 copy-done.1
  15.7 0.0 copy-start.2
  15.7 0.7 copy-done.2
  16.3 1.1 %bands.1 = (bf16[1280,384]{1,0:T(8,128)(2,1)S(1)}, f32[32,128]{1,0:T(8,128)S(1)}, f32[24,128]{1,0:T(8,128)S(1)}) custom-call(f32[10]{0:T(128)S(1)} %copy-done, s32[30]{0:T(128)S(1)} %copy-done.1, s32[3]{0:T(128)S(1)} %copy-done.2), custom_call_target="tpu_custom_call" | custom-call | flops 10000000 | bytes 2500000 | tf_op jit(solution)/shard_map/bands/pallas_call | solution.py:164
  17.4 6.3 %all-to-all-done = f32[32,8,128]{2,1,0:T(8,128)S(1)} async-done(((f32[32,8,128]{2,1,0:T(8,128)}), f32[32,8,128]{2,1,0:T(8,128)S(1)}, u32[]{:S(2)}, u32[]{:S(2)}) %all-to-all-start) | async-done | bytes 131104 | tf_op jit(solution)/shard_map/all_to_all | solution.py:193
  23.7 4.0 %collective-permute-start = (f32[256,128]{1,0:T(8,128)S(1)}, f32[256,128]{1,0:T(8,128)S(1)}, u32[]{:S(2)}, u32[]{:S(2)}) collective-permute-start(f32[256,128]{1,0:T(8,128)S(1)} %bitcast.2), channel_id=1, source_target_pairs={{1,0},{2,1},{3,2},{4,3},{5,4},{6,5},{7,6},{8,7},{9,8},{10,9},{11,1... | collective-permute-start | bytes 393224 | tf_op jit(solution)/shard_map/ppermute | solution.py:195
  27.7 3.1 %collective-permute-start.1 = (f32[256,128]{1,0:T(8,128)S(1)}, f32[256,128]{1,0:T(8,128)S(1)}, u32[]{:S(2)}, u32[]{:S(2)}) collective-permute-start(f32[256,128]{1,0:T(8,128)S(1)} %bitcast.3), channel_id=1, source_target_pairs={{0,1},{1,2},{2,3},{3,4},{4,5},{5,6},{6,7},{7,8},{8,9},{9,10},{10,1... | collective-permute-start | bytes 393224 | tf_op jit(solution)/shard_map/ppermute | solution.py:197
  30.8 1.3 %own.1 = (f32[10,384,256]{2,1,0:T(8,128)S(1)}, f32[32,128]{1,0:T(8,128)S(1)}) custom-call(f32[256,128]{1,0:T(8,128)S(1)} %bitcast.4, bf16[1280,384]{1,0:T(8,128)(2,1)S(1)} %get-tuple-element.17.xt_ref.refs_4_, f32[24,128]{1,0:T(8,128)S(1)} %get-tuple-element.18.level_ref.refs_5_), custom_call_target="tpu_custom_call" | custom-call | flops 750000000 | bytes 7000000 | tf_op jit(solution)/shard_map/own/pallas_call | solution.py:164
  32.1 0.0 collective-permute-done.right_ref
  32.1 0.9 %cross.1 = f32[32,1,128]{2,1,0:T(1,128)S(1)} custom-call(f32[256,128]{1,0:T(8,128)S(1)} %collective-permute-done.right_ref, bf16[1280,384]{1,0:T(8,128)(2,1)S(1)} %get-tuple-element.17.xt_ref.refs_4_, f32[24,128]{1,0:T(8,128)S(1)} %get-tuple-element.18.level_ref.refs_5_, f32[10,384,256]{2,1,0:T(8,128)S(1)} %get-tuple-element.19.b_ref, ...), custom_call_target="tpu_custom_call" | custom-call | flops 250000000 | bytes 5000000 | tf_op jit(solution)/shard_map/cross/pallas_call | solution.py:164
  33.0 11.6 %all_to_all.20.in_ref = f32[32,1,128]{2,1,0:T(1,128)S(1)} all-to-all(f32[32,1,128]{2,1,0:T(1,128)S(1)} %cross.1), channel_id=1, replica_groups=mesh['row'=32,'col'=16] {'row'}, dimensions={0} | all-to-all | bytes 32768 | tf_op jit(solution)/shard_map/all_to_all | solution.py:218
  44.6 0.6 regroup.1
  45.3 7.9 %all-to-all-start.2 = ((f32[16,1,128]{2,1,0:T(1,128)}), f32[16,1,128]{2,1,0:T(1,128)S(1)}, u32[]{:S(2)}, u32[]{:S(2)}) async-start(f32[16,1,128]{2,1,0:T(1,128)} %regroup.1), calls=%async_computation.2 | async-start | bytes 16384 | tf_op jit(solution)/shard_map/all_to_all | solution.py:220
  53.1 0.0 collective-permute-done.1.left_ref
  53.1 1.4 %along.1.refs_2_ = bf16[10,384,256]{2,1,0:T(8,128)(2,1)S(1)} custom-call(f32[256,128]{1,0:T(8,128)S(1)} %collective-permute-done.1.left_ref, f32[256,128]{1,0:T(8,128)S(1)} %bitcast.5, f32[256,128]{1,0:T(8,128)S(1)} %collective-permute-done.right_ref, bf16[1280,384]{1,0:T(8,128)(2,1)S(1)} %get-tuple-element.17.xt_ref.refs_4_, ...), custom_call_target="tpu_custom_call" | custom-call | flops 800000000 | bytes 4000000 | tf_op jit(solution)/shard_map/along/pallas_call | solution.py:164
  54.5 5.5 %all-to-all-done.2.refs_0_ = f32[16,1,128]{2,1,0:T(1,128)S(1)} async-done(((f32[16,1,128]{2,1,0:T(1,128)}), f32[16,1,128]{2,1,0:T(1,128)S(1)}, u32[]{:S(2)}, u32[]{:S(2)}) %all-to-all-start.2) | async-done | bytes 8224 | tf_op jit(solution)/shard_map/all_to_all | solution.py:220
  60.1 1.2 %combine.1 = (f32[30]{0:T(128)}, f32[256,128]{1,0:T(8,128)S(1)}) custom-call(f32[16,1,128]{2,1,0:T(1,128)S(1)} %all-to-all-done.2.refs_0_, f32[32,128]{1,0:T(8,128)S(1)} %get-tuple-element.21.refs_1_, bf16[10,384,256]{2,1,0:T(8,128)(2,1)S(1)} %along.1.refs_2_, f32[256,128]{1,0:T(8,128)S(1)} %bitcast.6, ...), custom_call_target="tpu_custom_call" | custom-call | flops 500000000 | bytes 5000000 | tf_op jit(solution)/shard_map/combine/pallas_call | solution.py:164
  61.3 12.4 %all_to_all.21 = f32[32,8,128]{2,1,0:T(8,128)S(1)} all-to-all(f32[32,8,128]{2,1,0:T(8,128)S(1)} %bitcast.7), channel_id=1, replica_groups=mesh['row'=32,'col'=16] {'row'}, dimensions={0} | all-to-all | bytes 262144 | tf_op jit(solution)/shard_map/all_to_all | solution.py:241
  73.7 0.7 copy.7
Async XLA Ops:
  0.6 23.1 %all-to-all-start = ((f32[32,8,128]{2,1,0:T(8,128)}), f32[32,8,128]{2,1,0:T(8,128)S(1)}, u32[]{:S(2)}, u32[]{:S(2)}) async-start(f32[32,8,128]{2,1,0:T(8,128)} %param.4), calls=%async_computation | async-start | bytes 262144 | tf_op jit(solution)/shard_map/all_to_all | solution.py:193
  14.4 0.7 copy-start
  15.0 0.7 copy-start.1
  15.7 0.7 copy-start.2
  23.7 8.4 %collective-permute-start = (f32[256,128]{1,0:T(8,128)S(1)}, f32[256,128]{1,0:T(8,128)S(1)}, u32[]{:S(2)}, u32[]{:S(2)}) collective-permute-start(f32[256,128]{1,0:T(8,128)S(1)} %bitcast.2), channel_id=1, source_target_pairs={{1,0},{2,1},{3,2},{4,3},{5,4},{6,5},{7,6},{8,7},{9,8},{10,9},{11,1... | collective-permute-start | bytes 393224 | tf_op jit(solution)/shard_map/ppermute | solution.py:195
  27.7 25.5 %collective-permute-start.1 = (f32[256,128]{1,0:T(8,128)S(1)}, f32[256,128]{1,0:T(8,128)S(1)}, u32[]{:S(2)}, u32[]{:S(2)}) collective-permute-start(f32[256,128]{1,0:T(8,128)S(1)} %bitcast.3), channel_id=1, source_target_pairs={{0,1},{1,2},{2,3},{3,4},{4,5},{5,6},{6,7},{7,8},{8,9},{9,10},{10,1... | collective-permute-start | bytes 393224 | tf_op jit(solution)/shard_map/ppermute | solution.py:197
  45.3 14.8 %all-to-all-start.2 = ((f32[16,1,128]{2,1,0:T(1,128)}), f32[16,1,128]{2,1,0:T(1,128)S(1)}, u32[]{:S(2)}, u32[]{:S(2)}) async-start(f32[16,1,128]{2,1,0:T(1,128)} %regroup.1), calls=%async_computation.2 | async-start | bytes 16384 | tf_op jit(solution)/shard_map/all_to_all | solution.py:220

commit v4 on v3

--- a/solution.py
+++ b/solution.py
@@ -208,17 +208,14 @@
     (part,) = call(
         cross_kernel,
         "cross",
-        (((rows, 1, 128), F32),),
+        (((cols, 1, 128), F32),),
         (right, xt, levels, b, own_rows_sum),
         scratch=(pltpu.VMEM((32, 128), F32),),
         flops=250_000_000,
         moved=5_000_000,
         special=100_000,
     )
-    part = lax.all_to_all(part, "row", split_axis=0, concat_axis=0, tiled=True)
-    (part,) = call(gather_kernel, "regroup", (((cols, 1, 128), F32),), (part,))
     part = lax.all_to_all(part, "col", split_axis=0, concat_axis=0, tiled=True)
-
     (a,) = call(
         along_kernel,
         "along",
@@ -229,6 +226,10 @@
         moved=4_000_000,
         special=300_000,
     )
+    part, a = lax.optimization_barrier((part, a))
+    (part,) = call(gather_kernel, "regroup", (((rows, 1, 128), F32),), (part,))
+    part = lax.all_to_all(part, "row", split_axis=0, concat_axis=0, tiled=True)
+
     compliance, sensitivity = call(
         lambda *refs: combine_kernel(cells, *refs),
         "combine",

time: 74.7 us -> 74 us (level); the launches traced: 74.3 us -> 72.9 us
  starting transfers between devices: 28.6 us -> 27.2 us
    all_to_all x1, starting transfers between devices: 7.86 us -> 6.43 us  [per_device(): part = lax.all_to_all(part, 'col', split_axis=0, concat_axis=0, tiled=True)]
where the time goes in v4:
time: 74 us; the launch traced here: 72.9 us
  starting transfers between devices  27.2 us (37%)
  blocking collectives  24 us (32%)
  waiting for transfers between devices  11.8 us (16%)
  Pallas kernels  6.51 us (9%)
  local copies, waits for them, and re-layouts  2.62 us (4%)
    all_to_all x1, starting transfers between devices, per_device(): lax.all_to_all(density, 'row', split_axis=0, concat_axis=0, tiled=True)  13.7 us
    all_to_all x1, blocking collectives, per_device(): lax.all_to_all(sensitivity.reshape(planes, own_rows, nx), 'row', split_ax...  12.4 us
    all_to_all x1, blocking collectives, per_device(): part = lax.all_to_all(part, 'row', split_axis=0, concat_axis=0, tiled=True)  11.6 us
    pallas_call x6, Pallas kernels, call(): pl.pallas_call(kernel, out_shape=tuple((jax.ShapeDtypeStruct(shape, dtype...  6.51 us
    all_to_all x1, starting transfers between devices, per_device(): part = lax.all_to_all(part, 'col', split_axis=0, concat_axis=0, tiled=True)  6.43 us
    all_to_all x1, waiting for transfers between devices, per_device(): lax.all_to_all(density, 'row', split_axis=0, concat_axis=0, tiled=True)  6.29 us
    all_to_all x1, waiting for transfers between devices, per_device(): part = lax.all_to_all(part, 'col', split_axis=0, concat_axis=0, tiled=True)  5.54 us
    ppermute x1, starting transfers between devices, per_device(): right = lax.ppermute(plane, 'col', [(i + 1, i) for i in range(cols - 1)])  3.96 us
  transfers between devices with their start and end apart: 4, of which 2 were waited for; matrix products, arithmetic and copies ran while one was open for 0% of the time, Pallas kernels for 7%

profile of v4, /device:TPU:1, one launch (start us, length us, event | category | flops | bytes accessed | tf_op | source)
XLA Modules:
  0.0 72.9 jit_solution(9909981437762339758)
XLA Ops:
  0.6 13.7 %all-to-all-start = ((f32[32,8,128]{2,1,0:T(8,128)}), f32[32,8,128]{2,1,0:T(8,128)S(1)}, u32[]{:S(2)}, u32[]{:S(2)}) async-start(f32[32,8,128]{2,1,0:T(8,128)} %param.4), calls=%async_computation | async-start | bytes 262144 | tf_op jit(solution)/shard_map/all_to_all | solution.py:193
  14.4 0.0 copy-start
  14.4 0.6 copy-done
  15.0 0.0 copy-start.1
  15.0 0.7 copy-done.1
  15.7 0.0 copy-start.2
  15.7 0.7 copy-done.2
  16.3 1.1 %bands.1 = (bf16[1280,384]{1,0:T(8,128)(2,1)S(1)}, f32[32,128]{1,0:T(8,128)S(1)}, f32[24,128]{1,0:T(8,128)S(1)}) custom-call(f32[10]{0:T(128)S(1)} %copy-done, s32[30]{0:T(128)S(1)} %copy-done.1, s32[3]{0:T(128)S(1)} %copy-done.2), custom_call_target="tpu_custom_call" | custom-call | flops 10000000 | bytes 2500000 | tf_op jit(solution)/shard_map/bands/pallas_call | solution.py:164
  17.4 6.3 %all-to-all-done = f32[32,8,128]{2,1,0:T(8,128)S(1)} async-done(((f32[32,8,128]{2,1,0:T(8,128)}), f32[32,8,128]{2,1,0:T(8,128)S(1)}, u32[]{:S(2)}, u32[]{:S(2)}) %all-to-all-start) | async-done | bytes 131104 | tf_op jit(solution)/shard_map/all_to_all | solution.py:193
  23.7 4.0 %collective-permute-start = (f32[256,128]{1,0:T(8,128)S(1)}, f32[256,128]{1,0:T(8,128)S(1)}, u32[]{:S(2)}, u32[]{:S(2)}) collective-permute-start(f32[256,128]{1,0:T(8,128)S(1)} %bitcast.2), channel_id=1, source_target_pairs={{1,0},{2,1},{3,2},{4,3},{5,4},{6,5},{7,6},{8,7},{9,8},{10,9},{11,1... | collective-permute-start | bytes 393224 | tf_op jit(solution)/shard_map/ppermute | solution.py:195
  27.7 3.1 %collective-permute-start.1 = (f32[256,128]{1,0:T(8,128)S(1)}, f32[256,128]{1,0:T(8,128)S(1)}, u32[]{:S(2)}, u32[]{:S(2)}) collective-permute-start(f32[256,128]{1,0:T(8,128)S(1)} %bitcast.3), channel_id=1, source_target_pairs={{0,1},{1,2},{2,3},{3,4},{4,5},{5,6},{6,7},{7,8},{8,9},{9,10},{10,1... | collective-permute-start | bytes 393224 | tf_op jit(solution)/shard_map/ppermute | solution.py:197
  30.8 1.3 %own.1 = (f32[10,384,256]{2,1,0:T(8,128)S(1)}, f32[32,128]{1,0:T(8,128)S(1)}) custom-call(f32[256,128]{1,0:T(8,128)S(1)} %bitcast.4, bf16[1280,384]{1,0:T(8,128)(2,1)S(1)} %get-tuple-element.19.xt_ref.refs_4_, f32[24,128]{1,0:T(8,128)S(1)} %get-tuple-element.20.level_ref.refs_5_), custom_call_target="tpu_custom_call" | custom-call | flops 750000000 | bytes 7000000 | tf_op jit(solution)/shard_map/own/pallas_call | solution.py:164
  32.1 0.0 collective-permute-done.right_ref
  32.1 1.5 %cross.1 = f32[16,1,128]{2,1,0:T(1,128)} custom-call(f32[256,128]{1,0:T(8,128)S(1)} %collective-permute-done.right_ref, bf16[1280,384]{1,0:T(8,128)(2,1)S(1)} %get-tuple-element.19.xt_ref.refs_4_, f32[24,128]{1,0:T(8,128)S(1)} %get-tuple-element.20.level_ref.refs_5_, f32[10,384,256]{2,1,0:T(8,128)S(1)} %get-tuple-element.21.b_ref, ...), custom_call_target="tpu_custom_call" | custom-call | flops 250000000 | bytes 5000000 | tf_op jit(solution)/shard_map/cross/pallas_call | solution.py:164
  33.6 6.4 %all-to-all-start.1 = ((f32[16,1,128]{2,1,0:T(1,128)}), f32[16,1,128]{2,1,0:T(1,128)S(1)}, u32[]{:S(2)}, u32[]{:S(2)}) async-start(f32[16,1,128]{2,1,0:T(1,128)} %cross.1), calls=%async_computation.1 | async-start | bytes 16384 | tf_op jit(solution)/shard_map/all_to_all | solution.py:218
  40.0 0.0 collective-permute-done.1.left_ref
  40.0 1.4 %along.1.refs_2_ = bf16[10,384,256]{2,1,0:T(8,128)(2,1)S(1)} custom-call(f32[256,128]{1,0:T(8,128)S(1)} %collective-permute-done.1.left_ref, f32[256,128]{1,0:T(8,128)S(1)} %bitcast.5, f32[256,128]{1,0:T(8,128)S(1)} %collective-permute-done.right_ref, bf16[1280,384]{1,0:T(8,128)(2,1)S(1)} %get-tuple-element.19.xt_ref.refs_4_, ...), custom_call_target="tpu_custom_call" | custom-call | flops 800000000 | bytes 4000000 | tf_op jit(solution)/shard_map/along/pallas_call | solution.py:164
  41.4 5.5 %all-to-all-done.1.in_ref = f32[16,1,128]{2,1,0:T(1,128)S(1)} async-done(((f32[16,1,128]{2,1,0:T(1,128)}), f32[16,1,128]{2,1,0:T(1,128)S(1)}, u32[]{:S(2)}, u32[]{:S(2)}) %all-to-all-start.1) | async-done | bytes 8224 | tf_op jit(solution)/shard_map/all_to_all | solution.py:218
  47.0 11.6 %all_to_all.20.refs_0_ = f32[32,1,128]{2,1,0:T(1,128)S(1)} all-to-all(f32[32,1,128]{2,1,0:T(1,128)S(1)} %regroup.1), channel_id=1, replica_groups=mesh['row'=32,'col'=16] {'row'}, dimensions={0} | all-to-all | bytes 32768 | tf_op jit(solution)/shard_map/all_to_all | solution.py:231
  58.6 1.2 %combine.1 = (f32[30]{0:T(128)}, f32[256,128]{1,0:T(8,128)S(1)}) custom-call(f32[32,1,128]{2,1,0:T(1,128)S(1)} %all_to_all.20.refs_0_, f32[32,128]{1,0:T(8,128)S(1)} %get-tuple-element.24.refs_1_, bf16[10,384,256]{2,1,0:T(8,128)(2,1)S(1)} %along.1.refs_2_, f32[256,128]{1,0:T(8,128)S(1)} %bitcast.6, bf16[1280,384]{1,0:T(8,128)(2,1)S(1)} %get-tuple-element.19.xt_ref.refs_4_, ...), custom_call_target="tpu_custom_call" | custom-call | flops 500000000 | bytes 5000000 | tf_op jit(solution)/shard_map/combine/pallas_call | solution.py:164
  59.9 12.4 %all_to_all.21 = f32[32,8,128]{2,1,0:T(8,128)S(1)} all-to-all(f32[32,8,128]{2,1,0:T(8,128)S(1)} %bitcast.7), channel_id=1, replica_groups=mesh['row'=32,'col'=16] {'row'}, dimensions={0} | all-to-all | bytes 262144 | tf_op jit(solution)/shard_map/all_to_all | solution.py:242
  72.2 0.7 copy.7
  (1 shorter events, 0.0 us)
Async XLA Ops:
  0.6 23.1 %all-to-all-start = ((f32[32,8,128]{2,1,0:T(8,128)}), f32[32,8,128]{2,1,0:T(8,128)S(1)}, u32[]{:S(2)}, u32[]{:S(2)}) async-start(f32[32,8,128]{2,1,0:T(8,128)} %param.4), calls=%async_computation | async-start | bytes 262144 | tf_op jit(solution)/shard_map/all_to_all | solution.py:193
  14.4 0.7 copy-start
  15.0 0.7 copy-start.1
  15.7 0.7 copy-start.2
  23.7 8.4 %collective-permute-start = (f32[256,128]{1,0:T(8,128)S(1)}, f32[256,128]{1,0:T(8,128)S(1)}, u32[]{:S(2)}, u32[]{:S(2)}) collective-permute-start(f32[256,128]{1,0:T(8,128)S(1)} %bitcast.2), channel_id=1, source_target_pairs={{1,0},{2,1},{3,2},{4,3},{5,4},{6,5},{7,6},{8,7},{9,8},{10,9},{11,1... | collective-permute-start | bytes 393224 | tf_op jit(solution)/shard_map/ppermute | solution.py:195
  27.7 12.3 %collective-permute-start.1 = (f32[256,128]{1,0:T(8,128)S(1)}, f32[256,128]{1,0:T(8,128)S(1)}, u32[]{:S(2)}, u32[]{:S(2)}) collective-permute-start(f32[256,128]{1,0:T(8,128)S(1)} %bitcast.3), channel_id=1, source_target_pairs={{0,1},{1,2},{2,3},{3,4},{4,5},{5,6},{6,7},{7,8},{8,9},{9,10},{10,1... | collective-permute-start | bytes 393224 | tf_op jit(solution)/shard_map/ppermute | solution.py:197
  33.6 13.4 %all-to-all-start.1 = ((f32[16,1,128]{2,1,0:T(1,128)}), f32[16,1,128]{2,1,0:T(1,128)S(1)}, u32[]{:S(2)}, u32[]{:S(2)}) async-start(f32[16,1,128]{2,1,0:T(1,128)} %cross.1), calls=%async_computation.1 | async-start | bytes 16384 | tf_op jit(solution)/shard_map/all_to_all | solution.py:218

commit v5 on v4

--- a/solution.py
+++ b/solution.py
@@ -1,3 +1,5 @@
+from functools import partial
+
 import jax
 import jax.numpy as jnp
 from jax import lax
@@ -17,6 +19,7 @@
 VMEM = pl.BlockSpec(memory_space=pltpu.VMEM)
 SMEM = pl.BlockSpec(memory_space=pltpu.SMEM)
 MIB = 1024 * 1024
+FIRST = {"row": 18, "col": 8}
 
 
 def bands_kernel(sigma_ref, width_ref, index_ref, xt_ref, member_ref, level_ref):
@@ -57,6 +60,21 @@
         level_ref[16 + v : 17 + v, :] = 1.0 / (low + high)
 
 
+def regroup(x, axis):
+    size = lax.axis_size(axis)
+    order = [(FIRST[axis] + i) % size for i in range(size)]
+    return lax.all_to_all(x, axis, split_axis=0, concat_axis=0, axis_index_groups=[order], tiled=True)
+
+
+def turned(x, rows):
+    rows %= x.shape[0]
+    return x if rows == 0 else jnp.concatenate([x[-rows:], x[:-rows]], axis=0)
+
+
+def columns(plane_ref, turn):
+    return turned(plane_ref[...], turn).T
+
+
 def column_to_row(column):
     rows = column.shape[0]
     at = lax.broadcasted_iota(jnp.int32, (rows, 128), 0) == lax.broadcasted_iota(jnp.int32, (rows, 128), 1)
@@ -78,9 +96,9 @@
     return jnp.concatenate([xt_ref[rows, HALF : 3 * HALF], xt_ref[rows, 0 : 2 * HALF]], axis=0)
 
 
-def own_kernel(own_ref, xt_ref, level_ref, b_ref, rows_ref, p_ref, a_ref):
+def own_kernel(turn, own_ref, xt_ref, level_ref, b_ref, rows_ref, p_ref, a_ref):
     ny = own_ref.shape[0]
-    own = own_ref[...].T
+    own = columns(own_ref, turn)
     for v in range(VARIANTS):
         level, low, inverse = constants(level_ref, v, ny)
         value, _ = project(own, level, low, inverse)
@@ -99,9 +117,9 @@
             rows_ref[v * WIDTHS + w : v * WIDTHS + w + 1, :] = line[:, 0:128] + line[:, 128:256]
 
 
-def cross_kernel(right_ref, xt_ref, level_ref, b_ref, own_rows_ref, part_ref, rows_ref):
+def cross_kernel(turn, right_ref, xt_ref, level_ref, b_ref, own_rows_ref, part_ref, rows_ref):
     ny = right_ref.shape[0]
-    right = right_ref[...].T
+    right = columns(right_ref, turn)
     rows_ref[...] = own_rows_ref[...]
     for v in range(VARIANTS):
         level, low, inverse = constants(level_ref, v, ny)
@@ -116,9 +134,9 @@
     part_ref[...] = jnp.broadcast_to(sums.reshape(1, 1, 128), part_ref.shape)
 
 
-def along_kernel(left_ref, own_ref, right_ref, xt_ref, level_ref, a_ref, p_ref):
+def along_kernel(turn, left_ref, own_ref, right_ref, xt_ref, level_ref, a_ref, p_ref):
     ny = left_ref.shape[0]
-    left, own, right = left_ref[...].T, own_ref[...].T, right_ref[...].T
+    left, own, right = [columns(ref, turn) for ref in (left_ref, own_ref, right_ref)]
     for v in range(VARIANTS):
         level, low, inverse = constants(level_ref, v, ny)
         p_ref[0:HALF, :] = project(left, level, low, inverse)[0]
@@ -133,7 +151,7 @@
     out_ref[...] = jnp.broadcast_to(total, out_ref.shape)
 
 
-def combine_kernel(cells, sums_ref, member_ref, a_ref, own_ref, xt_ref, level_ref, compliance_ref, out_ref, total_ref):
+def combine_kernel(cells, turn, sums_ref, member_ref, a_ref, own_ref, xt_ref, level_ref, compliance_ref, out_ref, total_ref):
     pairs = jnp.sum(sums_ref[...], axis=0) * (1.0 / cells)
     member = member_ref[...]
     compliance = jnp.sum(member * pairs, axis=1, keepdims=True)
@@ -150,14 +168,14 @@
             k = v * WIDTHS + w
             term = per_pair[:, k : k + 1] * field[v * HALF : (v + 1) * HALF, :]
             total_ref[v] = term if w == 0 else total_ref[v] + term
-    own = own_ref[...].T
+    own = columns(own_ref, turn)
     total = None
     for v in range(VARIANTS):
         level, low, inverse = constants(level_ref, v, own.shape[1])
         inner = jnp.tanh(SHARPNESS * (own - level))
         term = total_ref[v] * (SHARPNESS * (1.0 - inner * inner) * inverse)
         total = term if total is None else total + term
-    out_ref[...] = total.T
+    out_ref[...] = turned(total.T, -turn)
 
 
 def call(kernel, name, out, inputs, scratch=(), specs=None, flops=0, moved=0, special=0):
@@ -179,6 +197,7 @@
     ny = own_rows * rows
     cells = float(planes * ny * nx * cols)
     tall = VARIANTS * HALF
+    turn = FIRST["row"] * own_rows
 
     xt, member, levels = call(
         bands_kernel,
@@ -190,13 +209,13 @@
         moved=2_500_000,
         special=500_000,
     )
-    plane = lax.all_to_all(density, "row", split_axis=0, concat_axis=0, tiled=True).reshape(ny, nx)
+    plane = regroup(density, "row").reshape(ny, nx)
     plane, xt, member, levels = lax.optimization_barrier((plane, xt, member, levels))
     right = lax.ppermute(plane, "col", [(i + 1, i) for i in range(cols - 1)])
 
     left = lax.ppermute(plane, "col", [(i, i + 1) for i in range(cols - 1)])
     b, own_rows_sum = call(
-        own_kernel,
+        partial(own_kernel, turn),
         "own",
         (((WIDTHS, tall, ny), F32), ((32, 128), F32)),
         (plane, xt, levels),
@@ -206,7 +225,7 @@
         special=100_000,
     )
     (part,) = call(
-        cross_kernel,
+        partial(cross_kernel, turn),
         "cross",
         (((cols, 1, 128), F32),),
         (right, xt, levels, b, own_rows_sum),
@@ -215,9 +234,9 @@
         moved=5_000_000,
         special=100_000,
     )
-    part = lax.all_to_all(part, "col", split_axis=0, concat_axis=0, tiled=True)
+    part = regroup(part, "col")
     (a,) = call(
-        along_kernel,
+        partial(along_kernel, turn),
         "along",
         (((WIDTHS, tall, ny), BF16),),
         (left, plane, right, xt, levels),
@@ -228,10 +247,10 @@
     )
     part, a = lax.optimization_barrier((part, a))
     (part,) = call(gather_kernel, "regroup", (((rows, 1, 128), F32),), (part,))
-    part = lax.all_to_all(part, "row", split_axis=0, concat_axis=0, tiled=True)
+    part = regroup(part, "row")
 
     compliance, sensitivity = call(
-        lambda *refs: combine_kernel(cells, *refs),
+        partial(combine_kernel, cells, turn),
         "combine",
         (((CHANNELS,), F32), ((ny, nx), F32)),
         (part, member, a, plane, xt, levels),
@@ -239,9 +258,7 @@
         flops=500_000_000,
         moved=5_000_000,
     )
-    sensitivity = lax.all_to_all(
-        sensitivity.reshape(planes, own_rows, nx), "row", split_axis=0, concat_axis=0, tiled=True
-    )
+    sensitivity = regroup(sensitivity.reshape(planes, own_rows, nx), "row")
     return compliance, sensitivity
 
 

time: 74 us -> 68.7 us (0.928)
  the two profiles are of different devices: /device:TPU:1 before, /device:TPU:4 now
where the time goes in v5:
time: 68.7 us; the launch traced here: 68.3 us
  starting transfers between devices  28.3 us (41%)
  blocking collectives  26.5 us (39%)
  Pallas kernels  6.52 us (9%)
  waiting for transfers between devices  3.7 us (5%)
  local copies, waits for them, and re-layouts  2.62 us (4%)
  between operations  0.7 us (1%)
    all_to_all x2, blocking collectives, regroup(): lax.all_to_all(x, axis, split_axis=0, concat_axis=0, axis_index_groups=[o...  26.5 us
    all_to_all x2, starting transfers between devices, regroup(): lax.all_to_all(x, axis, split_axis=0, concat_axis=0, axis_index_groups=[o...  24 us
    pallas_call x6, Pallas kernels, call(): pl.pallas_call(kernel, out_shape=tuple((jax.ShapeDtypeStruct(shape, dtype...  6.52 us
    all_to_all x2, waiting for transfers between devices, regroup(): lax.all_to_all(x, axis, split_axis=0, concat_axis=0, axis_index_groups=[o...  3.7 us
    ppermute x1, starting transfers between devices, per_device(): left = lax.ppermute(plane, 'col', [(i, i + 1) for i in range(cols - 1)])  3.04 us
    unnamed x7, local copies, waits for them, and re-layouts  2.62 us
  transfers between devices with their start and end apart: 4, of which 2 were waited for; matrix products, arithmetic and copies ran while one was open for 0% of the time, Pallas kernels for 8%

profile of v5, /device:TPU:4, one launch (start us, length us, event | category | flops | bytes accessed | tf_op | source)
XLA Modules:
  0.0 68.3 jit_solution(16308535393015888431)
XLA Ops:
  0.6 14.4 %all-to-all-start = ((f32[32,8,128]{2,1,0:T(8,128)}), f32[32,8,128]{2,1,0:T(8,128)S(1)}, u32[]{:S(2)}, u32[]{:S(2)}) async-start(f32[32,8,128]{2,1,0:T(8,128)} %param.4), calls=%async_computation | async-start | bytes 262144 | tf_op jit(solution)/shard_map/all_to_all | solution.py:66
  15.0 0.0 copy-start
  15.0 0.6 copy-done
  15.7 0.0 copy-start.1
  15.7 0.7 copy-done.1
  16.3 0.0 copy-start.2
  16.3 0.7 copy-done.2
  17.0 1.1 %bands.1 = (bf16[1280,384]{1,0:T(8,128)(2,1)S(1)}, f32[32,128]{1,0:T(8,128)S(1)}, f32[24,128]{1,0:T(8,128)S(1)}) custom-call(f32[10]{0:T(128)S(1)} %copy-done, s32[30]{0:T(128)S(1)} %copy-done.1, s32[3]{0:T(128)S(1)} %copy-done.2), custom_call_target="tpu_custom_call" | custom-call | flops 10000000 | bytes 2500000 | tf_op jit(solution)/shard_map/bands/pallas_call | solution.py:182
  18.1 2.8 %all-to-all-done = f32[32,8,128]{2,1,0:T(8,128)S(1)} async-done(((f32[32,8,128]{2,1,0:T(8,128)}), f32[32,8,128]{2,1,0:T(8,128)S(1)}, u32[]{:S(2)}, u32[]{:S(2)}) %all-to-all-start) | async-done | bytes 131104 | tf_op jit(solution)/shard_map/all_to_all | solution.py:66
  20.9 1.3 %collective-permute-start = (f32[256,128]{1,0:T(8,128)S(1)}, f32[256,128]{1,0:T(8,128)S(1)}, u32[]{:S(2)}, u32[]{:S(2)}) collective-permute-start(f32[256,128]{1,0:T(8,128)S(1)} %bitcast.2), channel_id=1, source_target_pairs={{1,0},{2,1},{3,2},{4,3},{5,4},{6,5},{7,6},{8,7},{9,8},{10,9},{11,1... | collective-permute-start | bytes 393224 | tf_op jit(solution)/shard_map/ppermute | solution.py:214
  22.2 3.0 %collective-permute-start.1 = (f32[256,128]{1,0:T(8,128)S(1)}, f32[256,128]{1,0:T(8,128)S(1)}, u32[]{:S(2)}, u32[]{:S(2)}) collective-permute-start(f32[256,128]{1,0:T(8,128)S(1)} %bitcast.3), channel_id=1, source_target_pairs={{0,1},{1,2},{2,3},{3,4},{4,5},{5,6},{6,7},{7,8},{8,9},{9,10},{10,1... | collective-permute-start | bytes 393224 | tf_op jit(solution)/shard_map/ppermute | solution.py:216
  25.2 1.3 %own.1 = (f32[10,384,256]{2,1,0:T(8,128)S(1)}, f32[32,128]{1,0:T(8,128)S(1)}) custom-call(f32[256,128]{1,0:T(8,128)S(1)} %bitcast.4, bf16[1280,384]{1,0:T(8,128)(2,1)S(1)} %get-tuple-element.19.xt_ref, f32[24,128]{1,0:T(8,128)S(1)} %get-tuple-element.20.level_ref), custom_call_target="tpu_custom_call" | custom-call | flops 750000000 | bytes 7000000 | tf_op jit(solution)/shard_map/own/pallas_call | solution.py:182
  26.5 0.0 collective-permute-done.right_ref
  26.6 1.5 %cross.1 = f32[16,1,128]{2,1,0:T(1,128)} custom-call(f32[256,128]{1,0:T(8,128)S(1)} %collective-permute-done.right_ref, bf16[1280,384]{1,0:T(8,128)(2,1)S(1)} %get-tuple-element.19.xt_ref, f32[24,128]{1,0:T(8,128)S(1)} %get-tuple-element.20.level_ref, f32[10,384,256]{2,1,0:T(8,128)S(1)} %get-tuple-element.21.b_ref, f32[32,128]{1,0:T(8,128)S(1)} %get-tuple-element.22.own_rows_ref), custom_call_target="tpu_custom_call" | custom-call | flops 250000000 | bytes 5000000 | tf_op jit(solution)/shard_map/cross/pallas_call | solution.py:182
  28.0 9.6 %all-to-all-start.1 = ((f32[16,1,128]{2,1,0:T(1,128)}), f32[16,1,128]{2,1,0:T(1,128)S(1)}, u32[]{:S(2)}, u32[]{:S(2)}) async-start(f32[16,1,128]{2,1,0:T(1,128)} %cross.1), calls=%async_computation.1 | async-start | bytes 16384 | tf_op jit(solution)/shard_map/all_to_all | solution.py:66
  37.6 0.0 collective-permute-done.1.left_ref
  37.6 1.4 %along.1.a_ref = bf16[10,384,256]{2,1,0:T(8,128)(2,1)S(1)} custom-call(f32[256,128]{1,0:T(8,128)S(1)} %collective-permute-done.1.left_ref, f32[256,128]{1,0:T(8,128)S(1)} %bitcast.5, f32[256,128]{1,0:T(8,128)S(1)} %collective-permute-done.right_ref, bf16[1280,384]{1,0:T(8,128)(2,1)S(1)} %get-tuple-element.19.xt_ref, f32[24,128]{1,0:T(8,128)S(1)} %get-tuple-element.20.level_ref), custom_call_target="tpu_custom_call" | custom-call | flops 800000000 | bytes 4000000 | tf_op jit(solution)/shard_map/along/pallas_call | solution.py:182
  39.0 0.9 %all-to-all-done.1.in_ref = f32[16,1,128]{2,1,0:T(1,128)S(1)} async-done(((f32[16,1,128]{2,1,0:T(1,128)}), f32[16,1,128]{2,1,0:T(1,128)S(1)}, u32[]{:S(2)}, u32[]{:S(2)}) %all-to-all-start.1) | async-done | bytes 8224 | tf_op jit(solution)/shard_map/all_to_all | solution.py:66
  39.9 12.6 %all_to_all.20.sums_ref = f32[32,1,128]{2,1,0:T(1,128)S(1)} all-to-all(f32[32,1,128]{2,1,0:T(1,128)S(1)} %regroup.1), channel_id=1, replica_groups={{288,304,320,336,352,368,384,400,416,432,448,464,480,496,0,16,32,48,64,..., dimensions={0} | all-to-all | bytes 32768 | tf_op jit(solution)/shard_map/all_to_all | solution.py:66
  52.5 1.2 %combine.1 = (f32[30]{0:T(128)}, f32[256,128]{1,0:T(8,128)S(1)}) custom-call(f32[32,1,128]{2,1,0:T(1,128)S(1)} %all_to_all.20.sums_ref, f32[32,128]{1,0:T(8,128)S(1)} %get-tuple-element.24.member_ref, bf16[10,384,256]{2,1,0:T(8,128)(2,1)S(1)} %along.1.a_ref, f32[256,128]{1,0:T(8,128)S(1)} %bitcast.6, bf16[1280,384]{1,0:T(8,128)(2,1)S(1)} %get-tuple-element.19.xt_ref, ...), custom_call_target="tpu_custom_call" | custom-call | flops 500000000 | bytes 5000000 | tf_op jit(solution)/shard_map/combine/pallas_call | solution.py:182
  53.7 14.0 %all_to_all.21 = f32[32,8,128]{2,1,0:T(8,128)S(1)} all-to-all(f32[32,8,128]{2,1,0:T(8,128)S(1)} %bitcast.7), channel_id=1, replica_groups={{288,304,320,336,352,368,384,400,416,432,448,464,480,496,0,16,32,48,64,..., dimensions={0} | all-to-all | bytes 262144 | tf_op jit(solution)/shard_map/all_to_all | solution.py:66
  67.7 0.7 copy.7
  (1 shorter events, 0.0 us)
Async XLA Ops:
  0.6 20.3 %all-to-all-start = ((f32[32,8,128]{2,1,0:T(8,128)}), f32[32,8,128]{2,1,0:T(8,128)S(1)}, u32[]{:S(2)}, u32[]{:S(2)}) async-start(f32[32,8,128]{2,1,0:T(8,128)} %param.4), calls=%async_computation | async-start | bytes 262144 | tf_op jit(solution)/shard_map/all_to_all | solution.py:66
  15.0 0.7 copy-start
  15.7 0.7 copy-start.1
  16.3 0.7 copy-start.2
  20.9 5.7 %collective-permute-start = (f32[256,128]{1,0:T(8,128)S(1)}, f32[256,128]{1,0:T(8,128)S(1)}, u32[]{:S(2)}, u32[]{:S(2)}) collective-permute-start(f32[256,128]{1,0:T(8,128)S(1)} %bitcast.2), channel_id=1, source_target_pairs={{1,0},{2,1},{3,2},{4,3},{5,4},{6,5},{7,6},{8,7},{9,8},{10,9},{11,1... | collective-permute-start | bytes 393224 | tf_op jit(solution)/shard_map/ppermute | solution.py:214
  22.2 15.4 %collective-permute-start.1 = (f32[256,128]{1,0:T(8,128)S(1)}, f32[256,128]{1,0:T(8,128)S(1)}, u32[]{:S(2)}, u32[]{:S(2)}) collective-permute-start(f32[256,128]{1,0:T(8,128)S(1)} %bitcast.3), channel_id=1, source_target_pairs={{0,1},{1,2},{2,3},{3,4},{4,5},{5,6},{6,7},{7,8},{8,9},{9,10},{10,1... | collective-permute-start | bytes 393224 | tf_op jit(solution)/shard_map/ppermute | solution.py:216
  28.0 11.8 %all-to-all-start.1 = ((f32[16,1,128]{2,1,0:T(1,128)}), f32[16,1,128]{2,1,0:T(1,128)S(1)}, u32[]{:S(2)}, u32[]{:S(2)}) async-start(f32[16,1,128]{2,1,0:T(1,128)} %cross.1), calls=%async_computation.1 | async-start | bytes 16384 | tf_op jit(solution)/shard_map/all_to_all | solution.py:66

commit v6 on v5

--- a/solution.py
+++ b/solution.py
@@ -19,7 +19,7 @@
 VMEM = pl.BlockSpec(memory_space=pltpu.VMEM)
 SMEM = pl.BlockSpec(memory_space=pltpu.SMEM)
 MIB = 1024 * 1024
-FIRST = {"row": 18, "col": 8}
+FIRST = {"row": 22, "col": 9}
 
 
 def bands_kernel(sigma_ref, width_ref, index_ref, xt_ref, member_ref, level_ref):
@@ -227,14 +227,17 @@
     (part,) = call(
         partial(cross_kernel, turn),
         "cross",
-        (((cols, 1, 128), F32),),
+        (((rows, 1, 128), F32),),
         (right, xt, levels, b, own_rows_sum),
         scratch=(pltpu.VMEM((32, 128), F32),),
         flops=250_000_000,
         moved=5_000_000,
         special=100_000,
     )
+    part = regroup(part, "row")
+    (part,) = call(gather_kernel, "regroup", (((cols, 1, 128), F32),), (part,))
     part = regroup(part, "col")
+
     (a,) = call(
         partial(along_kernel, turn),
         "along",
@@ -245,10 +248,6 @@
         moved=4_000_000,
         special=300_000,
     )
-    part, a = lax.optimization_barrier((part, a))
-    (part,) = call(gather_kernel, "regroup", (((rows, 1, 128), F32),), (part,))
-    part = regroup(part, "row")
-
     compliance, sensitivity = call(
         partial(combine_kernel, cells, turn),
         "combine",

time: 68.7 us -> 68 us (0.990)
  the two profiles are of different devices: /device:TPU:4 before, /device:TPU:1 now
where the time goes in v6:
time: 68 us; the launch traced here: 67.7 us
  starting transfers between devices  31.3 us (46%)
  blocking collectives  24.8 us (36%)
  Pallas kernels  6.51 us (10%)
  local copies, waits for them, and re-layouts  2.62 us (4%)
  waiting for transfers between devices  1.75 us (3%)
  between operations  0.71 us (1%)
    all_to_all x2, blocking collectives, regroup(): lax.all_to_all(x, axis, split_axis=0, concat_axis=0, axis_index_groups=[o...  24.8 us
    all_to_all x2, starting transfers between devices, regroup(): lax.all_to_all(x, axis, split_axis=0, concat_axis=0, axis_index_groups=[o...  24.5 us
    pallas_call x6, Pallas kernels, call(): pl.pallas_call(kernel, out_shape=tuple((jax.ShapeDtypeStruct(shape, dtype...  6.51 us
    ppermute x1, starting transfers between devices, per_device(): right = lax.ppermute(plane, 'col', [(i + 1, i) for i in range(cols - 1)])  3.71 us
    ppermute x1, starting transfers between devices, per_device(): left = lax.ppermute(plane, 'col', [(i, i + 1) for i in range(cols - 1)])  3.1 us
    unnamed x7, local copies, waits for them, and re-layouts  2.62 us
    all_to_all x2, waiting for transfers between devices, regroup(): lax.all_to_all(x, axis, split_axis=0, concat_axis=0, axis_index_groups=[o...  1.74 us
  transfers between devices with their start and end apart: 4, of which 2 were waited for; matrix products, arithmetic and copies ran while one was open for 0% of the time, Pallas kernels for 8%

profile of v6, /device:TPU:1, one launch (start us, length us, event | category | flops | bytes accessed | tf_op | source)
XLA Modules:
  0.0 67.7 jit_solution(8894386383445478094)
XLA Ops:
  0.6 16.2 %all-to-all-start = ((f32[32,8,128]{2,1,0:T(8,128)}), f32[32,8,128]{2,1,0:T(8,128)S(1)}, u32[]{:S(2)}, u32[]{:S(2)}) async-start(f32[32,8,128]{2,1,0:T(8,128)} %param.4), calls=%async_computation | async-start | bytes 262144 | tf_op jit(solution)/shard_map/all_to_all | solution.py:66
  16.8 0.0 copy-start
  16.9 0.6 copy-done
  17.5 0.0 copy-start.1
  17.5 0.7 copy-done.1
  18.2 0.0 copy-start.2
  18.2 0.7 copy-done.2
  18.8 1.1 %bands.1 = (bf16[1280,384]{1,0:T(8,128)(2,1)S(1)}, f32[32,128]{1,0:T(8,128)S(1)}, f32[24,128]{1,0:T(8,128)S(1)}) custom-call(f32[10]{0:T(128)S(1)} %copy-done, s32[30]{0:T(128)S(1)} %copy-done.1, s32[3]{0:T(128)S(1)} %copy-done.2), custom_call_target="tpu_custom_call" | custom-call | flops 10000000 | bytes 2500000 | tf_op jit(solution)/shard_map/bands/pallas_call | solution.py:182
  19.9 0.8 %all-to-all-done = f32[32,8,128]{2,1,0:T(8,128)S(1)} async-done(((f32[32,8,128]{2,1,0:T(8,128)}), f32[32,8,128]{2,1,0:T(8,128)S(1)}, u32[]{:S(2)}, u32[]{:S(2)}) %all-to-all-start) | async-done | bytes 131104 | tf_op jit(solution)/shard_map/all_to_all | solution.py:66
  20.7 3.7 %collective-permute-start = (f32[256,128]{1,0:T(8,128)S(1)}, f32[256,128]{1,0:T(8,128)S(1)}, u32[]{:S(2)}, u32[]{:S(2)}) collective-permute-start(f32[256,128]{1,0:T(8,128)S(1)} %bitcast.2), channel_id=1, source_target_pairs={{1,0},{2,1},{3,2},{4,3},{5,4},{6,5},{7,6},{8,7},{9,8},{10,9},{11,1... | collective-permute-start | bytes 393224 | tf_op jit(solution)/shard_map/ppermute | solution.py:214
  24.4 3.1 %collective-permute-start.1 = (f32[256,128]{1,0:T(8,128)S(1)}, f32[256,128]{1,0:T(8,128)S(1)}, u32[]{:S(2)}, u32[]{:S(2)}) collective-permute-start(f32[256,128]{1,0:T(8,128)S(1)} %bitcast.3), channel_id=1, source_target_pairs={{0,1},{1,2},{2,3},{3,4},{4,5},{5,6},{6,7},{7,8},{8,9},{9,10},{10,1... | collective-permute-start | bytes 393224 | tf_op jit(solution)/shard_map/ppermute | solution.py:216
  27.5 1.3 %own.1 = (f32[10,384,256]{2,1,0:T(8,128)S(1)}, f32[32,128]{1,0:T(8,128)S(1)}) custom-call(f32[256,128]{1,0:T(8,128)S(1)} %bitcast.4, bf16[1280,384]{1,0:T(8,128)(2,1)S(1)} %get-tuple-element.17.xt_ref, f32[24,128]{1,0:T(8,128)S(1)} %get-tuple-element.18.level_ref), custom_call_target="tpu_custom_call" | custom-call | flops 750000000 | bytes 7000000 | tf_op jit(solution)/shard_map/own/pallas_call | solution.py:182
  28.9 0.0 collective-permute-done.right_ref
  28.9 0.9 %cross.1 = f32[32,1,128]{2,1,0:T(1,128)S(1)} custom-call(f32[256,128]{1,0:T(8,128)S(1)} %collective-permute-done.right_ref, bf16[1280,384]{1,0:T(8,128)(2,1)S(1)} %get-tuple-element.17.xt_ref, f32[24,128]{1,0:T(8,128)S(1)} %get-tuple-element.18.level_ref, f32[10,384,256]{2,1,0:T(8,128)S(1)} %get-tuple-element.19.b_ref, ...), custom_call_target="tpu_custom_call" | custom-call | flops 250000000 | bytes 5000000 | tf_op jit(solution)/shard_map/cross/pallas_call | solution.py:182
  29.7 11.4 %all_to_all.20.in_ref = f32[32,1,128]{2,1,0:T(1,128)S(1)} all-to-all(f32[32,1,128]{2,1,0:T(1,128)S(1)} %cross.1), channel_id=1, replica_groups={{352,368,384,400,416,432,448,464,480,496,0,16,32,48,64,80,96,112,128,14..., dimensions={0} | all-to-all | bytes 32768 | tf_op jit(solution)/shard_map/all_to_all | solution.py:66
  41.1 0.6 regroup.1
  41.7 8.2 %all-to-all-start.2 = ((f32[16,1,128]{2,1,0:T(1,128)}), f32[16,1,128]{2,1,0:T(1,128)S(1)}, u32[]{:S(2)}, u32[]{:S(2)}) async-start(f32[16,1,128]{2,1,0:T(1,128)} %regroup.1), calls=%async_computation.2 | async-start | bytes 16384 | tf_op jit(solution)/shard_map/all_to_all | solution.py:66
  50.0 0.0 collective-permute-done.1.left_ref
  50.0 1.4 %along.1.a_ref = bf16[10,384,256]{2,1,0:T(8,128)(2,1)S(1)} custom-call(f32[256,128]{1,0:T(8,128)S(1)} %collective-permute-done.1.left_ref, f32[256,128]{1,0:T(8,128)S(1)} %bitcast.5, f32[256,128]{1,0:T(8,128)S(1)} %collective-permute-done.right_ref, bf16[1280,384]{1,0:T(8,128)(2,1)S(1)} %get-tuple-element.17.xt_ref, f32[24,128]{1,0:T(8,128)S(1)} %get-tuple-element.18.level_ref), custom_call_target="tpu_custom_call" | custom-call | flops 800000000 | bytes 4000000 | tf_op jit(solution)/shard_map/along/pallas_call | solution.py:182
  51.4 0.9 %all-to-all-done.2.sums_ref = f32[16,1,128]{2,1,0:T(1,128)S(1)} async-done(((f32[16,1,128]{2,1,0:T(1,128)}), f32[16,1,128]{2,1,0:T(1,128)S(1)}, u32[]{:S(2)}, u32[]{:S(2)}) %all-to-all-start.2) | async-done | bytes 8224 | tf_op jit(solution)/shard_map/all_to_all | solution.py:66
  52.3 1.2 %combine.1 = (f32[30]{0:T(128)}, f32[256,128]{1,0:T(8,128)S(1)}) custom-call(f32[16,1,128]{2,1,0:T(1,128)S(1)} %all-to-all-done.2.sums_ref, f32[32,128]{1,0:T(8,128)S(1)} %get-tuple-element.21.member_ref, bf16[10,384,256]{2,1,0:T(8,128)(2,1)S(1)} %along.1.a_ref, f32[256,128]{1,0:T(8,128)S(1)} %bitcast.6, bf16[1280,384]{1,0:T(8,128)(2,1)S(1)} %get-tuple-element.17.xt_ref, ...), custom_call_target="tpu_custom_call" | custom-call | flops 500000000 | bytes 5000000 | tf_op jit(solution)/shard_map/combine/pallas_call | solution.py:182
  53.5 13.5 %all_to_all.21 = f32[32,8,128]{2,1,0:T(8,128)S(1)} all-to-all(f32[32,8,128]{2,1,0:T(8,128)S(1)} %bitcast.7), channel_id=1, replica_groups={{352,368,384,400,416,432,448,464,480,496,0,16,32,48,64,80,96,112,128,14..., dimensions={0} | all-to-all | bytes 262144 | tf_op jit(solution)/shard_map/all_to_all | solution.py:66
  67.0 0.7 copy.7
Async XLA Ops:
  0.6 20.1 %all-to-all-start = ((f32[32,8,128]{2,1,0:T(8,128)}), f32[32,8,128]{2,1,0:T(8,128)S(1)}, u32[]{:S(2)}, u32[]{:S(2)}) async-start(f32[32,8,128]{2,1,0:T(8,128)} %param.4), calls=%async_computation | async-start | bytes 262144 | tf_op jit(solution)/shard_map/all_to_all | solution.py:66
  16.8 0.7 copy-start
  17.5 0.7 copy-start.1
  18.2 0.7 copy-start.2
  20.7 8.2 %collective-permute-start = (f32[256,128]{1,0:T(8,128)S(1)}, f32[256,128]{1,0:T(8,128)S(1)}, u32[]{:S(2)}, u32[]{:S(2)}) collective-permute-start(f32[256,128]{1,0:T(8,128)S(1)} %bitcast.2), channel_id=1, source_target_pairs={{1,0},{2,1},{3,2},{4,3},{5,4},{6,5},{7,6},{8,7},{9,8},{10,9},{11,1... | collective-permute-start | bytes 393224 | tf_op jit(solution)/shard_map/ppermute | solution.py:214
  24.4 25.6 %collective-permute-start.1 = (f32[256,128]{1,0:T(8,128)S(1)}, f32[256,128]{1,0:T(8,128)S(1)}, u32[]{:S(2)}, u32[]{:S(2)}) collective-permute-start(f32[256,128]{1,0:T(8,128)S(1)} %bitcast.3), channel_id=1, source_target_pairs={{0,1},{1,2},{2,3},{3,4},{4,5},{5,6},{6,7},{7,8},{8,9},{9,10},{10,1... | collective-permute-start | bytes 393224 | tf_op jit(solution)/shard_map/ppermute | solution.py:216
  41.7 10.6 %all-to-all-start.2 = ((f32[16,1,128]{2,1,0:T(1,128)}), f32[16,1,128]{2,1,0:T(1,128)S(1)}, u32[]{:S(2)}, u32[]{:S(2)}) async-start(f32[16,1,128]{2,1,0:T(1,128)} %regroup.1), calls=%async_computation.2 | async-start | bytes 16384 | tf_op jit(solution)/shard_map/all_to_all | solution.py:66

commit v7 on v6

--- a/solution.py
+++ b/solution.py
@@ -19,6 +19,7 @@
 VMEM = pl.BlockSpec(memory_space=pltpu.VMEM)
 SMEM = pl.BlockSpec(memory_space=pltpu.SMEM)
 MIB = 1024 * 1024
+SCALE = 1024.0
 FIRST = {"row": 22, "col": 9}
 
 
@@ -75,6 +76,21 @@
     return turned(plane_ref[...], turn).T
 
 
+def encode(x):
+    power = x * SCALE
+    for _ in range(3):
+        power = power * power
+    return jnp.where(x < 0.0, -power, power).astype(BF16)
+
+
+def decode(code):
+    power = code.astype(F32)
+    root = jnp.abs(power)
+    for _ in range(3):
+        root = jnp.sqrt(root)
+    return jnp.where(power < 0.0, -root, root) * (1.0 / SCALE)
+
+
 def column_to_row(column):
     rows = column.shape[0]
     at = lax.broadcasted_iota(jnp.int32, (rows, 128), 0) == lax.broadcasted_iota(jnp.int32, (rows, 128), 1)
@@ -175,7 +191,7 @@
         inner = jnp.tanh(SHARPNESS * (own - level))
         term = total_ref[v] * (SHARPNESS * (1.0 - inner * inner) * inverse)
         total = term if total is None else total + term
-    out_ref[...] = turned(total.T, -turn)
+    out_ref[...] = encode(turned(total.T, -turn))
 
 
 def call(kernel, name, out, inputs, scratch=(), specs=None, flops=0, moved=0, special=0):
@@ -251,13 +267,13 @@
     compliance, sensitivity = call(
         partial(combine_kernel, cells, turn),
         "combine",
-        (((CHANNELS,), F32), ((ny, nx), F32)),
+        (((CHANNELS,), F32), ((ny, nx), BF16)),
         (part, member, a, plane, xt, levels),
         scratch=(pltpu.VMEM((VARIANTS, HALF, ny), F32),),
         flops=500_000_000,
         moved=5_000_000,
     )
-    sensitivity = regroup(sensitivity.reshape(planes, own_rows, nx), "row")
+    sensitivity = decode(regroup(sensitivity.reshape(planes, own_rows, nx), "row"))
     return compliance, sensitivity
 
 

time: 68 us -> 67.1 us (0.987)
  blocking collectives: 24.8 us -> 23.8 us
  other arithmetic: 0 us -> 0.78 us
    all_to_all x2, blocking collectives: 24.8 us -> 23.8 us  [regroup(): lax.all_to_all(x, axis, split_axis=0, concat_axis=0, axis_index_groups=[o...]
    mul x0 -> x1, other arithmetic: none -> 0.78 us  [decode(): return jnp.where(power < 0.0, -root, root) * (1.0 / SCALE)]
    unnamed x7 -> x6, local copies, waits for them, and re-layouts: 2.62 us -> 1.96 us
where the time goes in v7:
time: 67.1 us; the launch traced here: 66.8 us
  starting transfers between devices  31.3 us (47%)
  blocking collectives  23.8 us (35%)
  Pallas kernels  6.51 us (10%)
  local copies, waits for them, and re-layouts  1.96 us (3%)
  waiting for transfers between devices  1.75 us (3%)
  other arithmetic  0.78 us (1%)
  between operations  0.71 us (1%)
    all_to_all x2, starting transfers between devices, regroup(): lax.all_to_all(x, axis, split_axis=0, concat_axis=0, axis_index_groups=[o...  24.5 us
    all_to_all x2, blocking collectives, regroup(): lax.all_to_all(x, axis, split_axis=0, concat_axis=0, axis_index_groups=[o...  23.8 us
    pallas_call x6, Pallas kernels, call(): pl.pallas_call(kernel, out_shape=tuple((jax.ShapeDtypeStruct(shape, dtype...  6.51 us
    ppermute x1, starting transfers between devices, per_device(): right = lax.ppermute(plane, 'col', [(i + 1, i) for i in range(cols - 1)])  3.71 us
    ppermute x1, starting transfers between devices, per_device(): left = lax.ppermute(plane, 'col', [(i, i + 1) for i in range(cols - 1)])  3.1 us
    unnamed x6, local copies, waits for them, and re-layouts  1.96 us
    all_to_all x2, waiting for transfers between devices, regroup(): lax.all_to_all(x, axis, split_axis=0, concat_axis=0, axis_index_groups=[o...  1.74 us
  transfers between devices with their start and end apart: 4, of which 2 were waited for; matrix products, arithmetic and copies ran while one was open for 0% of the time, Pallas kernels for 8%

profile of v7, /device:TPU:1, one launch (start us, length us, event | category | flops | bytes accessed | tf_op | source)
XLA Modules:
  0.0 66.8 jit_solution(3211440328872906693)
XLA Ops:
  0.6 16.2 %all-to-all-start = ((f32[32,8,128]{2,1,0:T(8,128)}), f32[32,8,128]{2,1,0:T(8,128)S(1)}, u32[]{:S(2)}, u32[]{:S(2)}) async-start(f32[32,8,128]{2,1,0:T(8,128)} %param.4), calls=%async_computation | async-start | bytes 262144 | tf_op jit(solution)/shard_map/all_to_all | solution.py:67
  16.8 0.0 copy-start
  16.9 0.6 copy-done
  17.5 0.0 copy-start.1
  17.5 0.7 copy-done.1
  18.2 0.0 copy-start.2
  18.2 0.7 copy-done.2
  18.8 1.1 %bands.1 = (bf16[1280,384]{1,0:T(8,128)(2,1)S(1)}, f32[32,128]{1,0:T(8,128)S(1)}, f32[24,128]{1,0:T(8,128)S(1)}) custom-call(f32[10]{0:T(128)S(1)} %copy-done, s32[30]{0:T(128)S(1)} %copy-done.1, s32[3]{0:T(128)S(1)} %copy-done.2), custom_call_target="tpu_custom_call" | custom-call | flops 10000000 | bytes 2500000 | tf_op jit(solution)/shard_map/bands/pallas_call | solution.py:198
  19.9 0.8 %all-to-all-done = f32[32,8,128]{2,1,0:T(8,128)S(1)} async-done(((f32[32,8,128]{2,1,0:T(8,128)}), f32[32,8,128]{2,1,0:T(8,128)S(1)}, u32[]{:S(2)}, u32[]{:S(2)}) %all-to-all-start) | async-done | bytes 131104 | tf_op jit(solution)/shard_map/all_to_all | solution.py:67
  20.7 3.7 %collective-permute-start = (f32[256,128]{1,0:T(8,128)S(1)}, f32[256,128]{1,0:T(8,128)S(1)}, u32[]{:S(2)}, u32[]{:S(2)}) collective-permute-start(f32[256,128]{1,0:T(8,128)S(1)} %bitcast.2), channel_id=1, source_target_pairs={{1,0},{2,1},{3,2},{4,3},{5,4},{6,5},{7,6},{8,7},{9,8},{10,9},{11,1... | collective-permute-start | bytes 393224 | tf_op jit(solution)/shard_map/ppermute | solution.py:230
  24.4 3.1 %collective-permute-start.1 = (f32[256,128]{1,0:T(8,128)S(1)}, f32[256,128]{1,0:T(8,128)S(1)}, u32[]{:S(2)}, u32[]{:S(2)}) collective-permute-start(f32[256,128]{1,0:T(8,128)S(1)} %bitcast.3), channel_id=1, source_target_pairs={{0,1},{1,2},{2,3},{3,4},{4,5},{5,6},{6,7},{7,8},{8,9},{9,10},{10,1... | collective-permute-start | bytes 393224 | tf_op jit(solution)/shard_map/ppermute | solution.py:232
  27.5 1.3 %own.1 = (f32[10,384,256]{2,1,0:T(8,128)S(1)}, f32[32,128]{1,0:T(8,128)S(1)}) custom-call(f32[256,128]{1,0:T(8,128)S(1)} %bitcast.4, bf16[1280,384]{1,0:T(8,128)(2,1)S(1)} %get-tuple-element.17.xt_ref, f32[24,128]{1,0:T(8,128)S(1)} %get-tuple-element.18.level_ref), custom_call_target="tpu_custom_call" | custom-call | flops 750000000 | bytes 7000000 | tf_op jit(solution)/shard_map/own/pallas_call | solution.py:198
  28.9 0.0 collective-permute-done.right_ref
  28.9 0.9 %cross.1 = f32[32,1,128]{2,1,0:T(1,128)S(1)} custom-call(f32[256,128]{1,0:T(8,128)S(1)} %collective-permute-done.right_ref, bf16[1280,384]{1,0:T(8,128)(2,1)S(1)} %get-tuple-element.17.xt_ref, f32[24,128]{1,0:T(8,128)S(1)} %get-tuple-element.18.level_ref, f32[10,384,256]{2,1,0:T(8,128)S(1)} %get-tuple-element.19.b_ref, ...), custom_call_target="tpu_custom_call" | custom-call | flops 250000000 | bytes 5000000 | tf_op jit(solution)/shard_map/cross/pallas_call | solution.py:198
  29.7 11.4 %all_to_all.20.in_ref = f32[32,1,128]{2,1,0:T(1,128)S(1)} all-to-all(f32[32,1,128]{2,1,0:T(1,128)S(1)} %cross.1), channel_id=1, replica_groups={{352,368,384,400,416,432,448,464,480,496,0,16,32,48,64,80,96,112,128,14..., dimensions={0} | all-to-all | bytes 32768 | tf_op jit(solution)/shard_map/all_to_all | solution.py:67
  41.1 0.6 regroup.1
  41.7 8.2 %all-to-all-start.2 = ((f32[16,1,128]{2,1,0:T(1,128)}), f32[16,1,128]{2,1,0:T(1,128)S(1)}, u32[]{:S(2)}, u32[]{:S(2)}) async-start(f32[16,1,128]{2,1,0:T(1,128)} %regroup.1), calls=%async_computation.2 | async-start | bytes 16384 | tf_op jit(solution)/shard_map/all_to_all | solution.py:67
  50.0 0.0 collective-permute-done.1.left_ref
  50.0 1.4 %along.1.a_ref = bf16[10,384,256]{2,1,0:T(8,128)(2,1)S(1)} custom-call(f32[256,128]{1,0:T(8,128)S(1)} %collective-permute-done.1.left_ref, f32[256,128]{1,0:T(8,128)S(1)} %bitcast.5, f32[256,128]{1,0:T(8,128)S(1)} %collective-permute-done.right_ref, bf16[1280,384]{1,0:T(8,128)(2,1)S(1)} %get-tuple-element.17.xt_ref, f32[24,128]{1,0:T(8,128)S(1)} %get-tuple-element.18.level_ref), custom_call_target="tpu_custom_call" | custom-call | flops 800000000 | bytes 4000000 | tf_op jit(solution)/shard_map/along/pallas_call | solution.py:198
  51.4 0.9 %all-to-all-done.2.sums_ref = f32[16,1,128]{2,1,0:T(1,128)S(1)} async-done(((f32[16,1,128]{2,1,0:T(1,128)}), f32[16,1,128]{2,1,0:T(1,128)S(1)}, u32[]{:S(2)}, u32[]{:S(2)}) %all-to-all-start.2) | async-done | bytes 8224 | tf_op jit(solution)/shard_map/all_to_all | solution.py:67
  52.3 1.2 %combine.1 = (f32[30]{0:T(128)}, bf16[256,128]{1,0:T(8,128)(2,1)S(1)}) custom-call(f32[16,1,128]{2,1,0:T(1,128)S(1)} %all-to-all-done.2.sums_ref, f32[32,128]{1,0:T(8,128)S(1)} %get-tuple-element.21.member_ref, bf16[10,384,256]{2,1,0:T(8,128)(2,1)S(1)} %along.1.a_ref, f32[256,128]{1,0:T(8,128)S(1)} %bitcast.6, ...), custom_call_target="tpu_custom_call" | custom-call | flops 500000000 | bytes 5000000 | tf_op jit(solution)/shard_map/combine/pallas_call | solution.py:198
  53.5 12.4 %all_to_all.21 = bf16[32,8,128]{2,1,0:T(8,128)(2,1)S(1)} all-to-all(bf16[32,8,128]{2,1,0:T(8,128)(2,1)S(1)} %bitcast.7), channel_id=1, replica_groups={{352,368,384,400,416,432,448,464,480,496,0,16,32,48,64,80,96,112,128,14..., dimensions={0} | all-to-all | bytes 131072 | tf_op jit(solution)/shard_map/all_to_all | solution.py:67
  66.0 0.8 %fusion.3 = f32[32,8,128]{2,1,0:T(8,128)} fusion(bf16[32,8,128]{2,1,0:T(8,128)(2,1)S(1)} %all_to_all.21), kind=kLoop, calls=%fused_computation.6 | loop fusion | flops 196608 | bytes 196608 | tf_op jit(solution)/shard_map/mul | solution.py:91
Async XLA Ops:
  0.6 20.1 %all-to-all-start = ((f32[32,8,128]{2,1,0:T(8,128)}), f32[32,8,128]{2,1,0:T(8,128)S(1)}, u32[]{:S(2)}, u32[]{:S(2)}) async-start(f32[32,8,128]{2,1,0:T(8,128)} %param.4), calls=%async_computation | async-start | bytes 262144 | tf_op jit(solution)/shard_map/all_to_all | solution.py:67
  16.8 0.7 copy-start
  17.5 0.7 copy-start.1
  18.2 0.7 copy-start.2
  20.7 8.2 %collective-permute-start = (f32[256,128]{1,0:T(8,128)S(1)}, f32[256,128]{1,0:T(8,128)S(1)}, u32[]{:S(2)}, u32[]{:S(2)}) collective-permute-start(f32[256,128]{1,0:T(8,128)S(1)} %bitcast.2), channel_id=1, source_target_pairs={{1,0},{2,1},{3,2},{4,3},{5,4},{6,5},{7,6},{8,7},{9,8},{10,9},{11,1... | collective-permute-start | bytes 393224 | tf_op jit(solution)/shard_map/ppermute | solution.py:230
  24.4 25.6 %collective-permute-start.1 = (f32[256,128]{1,0:T(8,128)S(1)}, f32[256,128]{1,0:T(8,128)S(1)}, u32[]{:S(2)}, u32[]{:S(2)}) collective-permute-start(f32[256,128]{1,0:T(8,128)S(1)} %bitcast.3), channel_id=1, source_target_pairs={{0,1},{1,2},{2,3},{3,4},{4,5},{5,6},{6,7},{7,8},{8,9},{9,10},{10,1... | collective-permute-start | bytes 393224 | tf_op jit(solution)/shard_map/ppermute | solution.py:232
  41.7 10.6 %all-to-all-start.2 = ((f32[16,1,128]{2,1,0:T(1,128)}), f32[16,1,128]{2,1,0:T(1,128)S(1)}, u32[]{:S(2)}, u32[]{:S(2)}) async-start(f32[16,1,128]{2,1,0:T(1,128)} %regroup.1), calls=%async_computation.2 | async-start | bytes 16384 | tf_op jit(solution)/shard_map/all_to_all | solution.py:67

commit v8 on v7

--- a/solution.py
+++ b/solution.py
@@ -20,7 +20,7 @@
 SMEM = pl.BlockSpec(memory_space=pltpu.SMEM)
 MIB = 1024 * 1024
 SCALE = 1024.0
-FIRST = {"row": 22, "col": 9}
+FIRST = {"row": 23, "col": 9}
 
 
 def bands_kernel(sigma_ref, width_ref, index_ref, xt_ref, member_ref, level_ref):

time: 67.1 us -> 68 us (1.013)
  waiting for transfers between devices: 1.75 us -> 2.62 us
    all_to_all x2, waiting for transfers between devices: 1.74 us -> 2.61 us  [regroup(): lax.all_to_all(x, axis, split_axis=0, concat_axis=0, axis_index_groups=[o...]
where the time goes in v8:
time: 68 us; the launch traced here: 67.7 us
  starting transfers between devices  31.1 us (46%)
  blocking collectives  24 us (35%)
  Pallas kernels  6.51 us (10%)
  waiting for transfers between devices  2.62 us (4%)
  local copies, waits for them, and re-layouts  1.96 us (3%)
  other arithmetic  0.78 us (1%)
  between operations  0.71 us (1%)
    all_to_all x2, starting transfers between devices, regroup(): lax.all_to_all(x, axis, split_axis=0, concat_axis=0, axis_index_groups=[o...  24.4 us
    all_to_all x2, blocking collectives, regroup(): lax.all_to_all(x, axis, split_axis=0, concat_axis=0, axis_index_groups=[o...  24 us
    pallas_call x6, Pallas kernels, call(): pl.pallas_call(kernel, out_shape=tuple((jax.ShapeDtypeStruct(shape, dtype...  6.51 us
    ppermute x1, starting transfers between devices, per_device(): right = lax.ppermute(plane, 'col', [(i + 1, i) for i in range(cols - 1)])  3.65 us
    ppermute x1, starting transfers between devices, per_device(): left = lax.ppermute(plane, 'col', [(i, i + 1) for i in range(cols - 1)])  3.1 us
    all_to_all x2, waiting for transfers between devices, regroup(): lax.all_to_all(x, axis, split_axis=0, concat_axis=0, axis_index_groups=[o...  2.61 us
    unnamed x6, local copies, waits for them, and re-layouts  1.96 us
  transfers between devices with their start and end apart: 4, of which 2 were waited for; matrix products, arithmetic and copies ran while one was open for 0% of the time, Pallas kernels for 8%

profile of v8, /device:TPU:1, one launch (start us, length us, event | category | flops | bytes accessed | tf_op | source)
XLA Modules:
  0.0 67.7 jit_solution(15085811242307951085)
XLA Ops:
  0.6 16.2 %all-to-all-start = ((f32[32,8,128]{2,1,0:T(8,128)}), f32[32,8,128]{2,1,0:T(8,128)S(1)}, u32[]{:S(2)}, u32[]{:S(2)}) async-start(f32[32,8,128]{2,1,0:T(8,128)} %param.4), calls=%async_computation | async-start | bytes 262144 | tf_op jit(solution)/shard_map/all_to_all | solution.py:67
  16.8 0.0 copy-start
  16.8 0.6 copy-done
  17.4 0.0 copy-start.1
  17.4 0.7 copy-done.1
  18.1 0.0 copy-start.2
  18.1 0.7 copy-done.2
  18.8 1.1 %bands.1 = (bf16[1280,384]{1,0:T(8,128)(2,1)S(1)}, f32[32,128]{1,0:T(8,128)S(1)}, f32[24,128]{1,0:T(8,128)S(1)}) custom-call(f32[10]{0:T(128)S(1)} %copy-done, s32[30]{0:T(128)S(1)} %copy-done.1, s32[3]{0:T(128)S(1)} %copy-done.2), custom_call_target="tpu_custom_call" | custom-call | flops 10000000 | bytes 2500000 | tf_op jit(solution)/shard_map/bands/pallas_call | solution.py:198
  19.8 1.7 %all-to-all-done = f32[32,8,128]{2,1,0:T(8,128)S(1)} async-done(((f32[32,8,128]{2,1,0:T(8,128)}), f32[32,8,128]{2,1,0:T(8,128)S(1)}, u32[]{:S(2)}, u32[]{:S(2)}) %all-to-all-start) | async-done | bytes 131104 | tf_op jit(solution)/shard_map/all_to_all | solution.py:67
  21.5 3.7 %collective-permute-start = (f32[256,128]{1,0:T(8,128)S(1)}, f32[256,128]{1,0:T(8,128)S(1)}, u32[]{:S(2)}, u32[]{:S(2)}) collective-permute-start(f32[256,128]{1,0:T(8,128)S(1)} %bitcast.2), channel_id=1, source_target_pairs={{1,0},{2,1},{3,2},{4,3},{5,4},{6,5},{7,6},{8,7},{9,8},{10,9},{11,1... | collective-permute-start | bytes 393224 | tf_op jit(solution)/shard_map/ppermute | solution.py:230
  25.2 3.1 %collective-permute-start.1 = (f32[256,128]{1,0:T(8,128)S(1)}, f32[256,128]{1,0:T(8,128)S(1)}, u32[]{:S(2)}, u32[]{:S(2)}) collective-permute-start(f32[256,128]{1,0:T(8,128)S(1)} %bitcast.3), channel_id=1, source_target_pairs={{0,1},{1,2},{2,3},{3,4},{4,5},{5,6},{6,7},{7,8},{8,9},{9,10},{10,1... | collective-permute-start | bytes 393224 | tf_op jit(solution)/shard_map/ppermute | solution.py:232
  28.3 1.3 %own.1 = (f32[10,384,256]{2,1,0:T(8,128)S(1)}, f32[32,128]{1,0:T(8,128)S(1)}) custom-call(f32[256,128]{1,0:T(8,128)S(1)} %bitcast.4, bf16[1280,384]{1,0:T(8,128)(2,1)S(1)} %get-tuple-element.17.xt_ref, f32[24,128]{1,0:T(8,128)S(1)} %get-tuple-element.18.level_ref), custom_call_target="tpu_custom_call" | custom-call | flops 750000000 | bytes 7000000 | tf_op jit(solution)/shard_map/own/pallas_call | solution.py:198
  29.6 0.0 collective-permute-done.right_ref
  29.6 0.9 %cross.1 = f32[32,1,128]{2,1,0:T(1,128)S(1)} custom-call(f32[256,128]{1,0:T(8,128)S(1)} %collective-permute-done.right_ref, bf16[1280,384]{1,0:T(8,128)(2,1)S(1)} %get-tuple-element.17.xt_ref, f32[24,128]{1,0:T(8,128)S(1)} %get-tuple-element.18.level_ref, f32[10,384,256]{2,1,0:T(8,128)S(1)} %get-tuple-element.19.b_ref, ...), custom_call_target="tpu_custom_call" | custom-call | flops 250000000 | bytes 5000000 | tf_op jit(solution)/shard_map/cross/pallas_call | solution.py:198
  30.5 11.5 %all_to_all.20.in_ref = f32[32,1,128]{2,1,0:T(1,128)S(1)} all-to-all(f32[32,1,128]{2,1,0:T(1,128)S(1)} %cross.1), channel_id=1, replica_groups={{368,384,400,416,432,448,464,480,496,0,16,32,48,64,80,96,112,128,144,16..., dimensions={0} | all-to-all | bytes 32768 | tf_op jit(solution)/shard_map/all_to_all | solution.py:67
  42.0 0.6 regroup.1
  42.7 8.2 %all-to-all-start.2 = ((f32[16,1,128]{2,1,0:T(1,128)}), f32[16,1,128]{2,1,0:T(1,128)S(1)}, u32[]{:S(2)}, u32[]{:S(2)}) async-start(f32[16,1,128]{2,1,0:T(1,128)} %regroup.1), calls=%async_computation.2 | async-start | bytes 16384 | tf_op jit(solution)/shard_map/all_to_all | solution.py:67
  50.9 0.0 collective-permute-done.1.left_ref
  50.9 1.4 %along.1.a_ref = bf16[10,384,256]{2,1,0:T(8,128)(2,1)S(1)} custom-call(f32[256,128]{1,0:T(8,128)S(1)} %collective-permute-done.1.left_ref, f32[256,128]{1,0:T(8,128)S(1)} %bitcast.5, f32[256,128]{1,0:T(8,128)S(1)} %collective-permute-done.right_ref, bf16[1280,384]{1,0:T(8,128)(2,1)S(1)} %get-tuple-element.17.xt_ref, f32[24,128]{1,0:T(8,128)S(1)} %get-tuple-element.18.level_ref), custom_call_target="tpu_custom_call" | custom-call | flops 800000000 | bytes 4000000 | tf_op jit(solution)/shard_map/along/pallas_call | solution.py:198
  52.3 0.9 %all-to-all-done.2.sums_ref = f32[16,1,128]{2,1,0:T(1,128)S(1)} async-done(((f32[16,1,128]{2,1,0:T(1,128)}), f32[16,1,128]{2,1,0:T(1,128)S(1)}, u32[]{:S(2)}, u32[]{:S(2)}) %all-to-all-start.2) | async-done | bytes 8224 | tf_op jit(solution)/shard_map/all_to_all | solution.py:67
  53.2 1.2 %combine.1 = (f32[30]{0:T(128)}, bf16[256,128]{1,0:T(8,128)(2,1)S(1)}) custom-call(f32[16,1,128]{2,1,0:T(1,128)S(1)} %all-to-all-done.2.sums_ref, f32[32,128]{1,0:T(8,128)S(1)} %get-tuple-element.21.member_ref, bf16[10,384,256]{2,1,0:T(8,128)(2,1)S(1)} %along.1.a_ref, f32[256,128]{1,0:T(8,128)S(1)} %bitcast.6, ...), custom_call_target="tpu_custom_call" | custom-call | flops 500000000 | bytes 5000000 | tf_op jit(solution)/shard_map/combine/pallas_call | solution.py:198
  54.4 12.4 %all_to_all.21 = bf16[32,8,128]{2,1,0:T(8,128)(2,1)S(1)} all-to-all(bf16[32,8,128]{2,1,0:T(8,128)(2,1)S(1)} %bitcast.7), channel_id=1, replica_groups={{368,384,400,416,432,448,464,480,496,0,16,32,48,64,80,96,112,128,144,16..., dimensions={0} | all-to-all | bytes 131072 | tf_op jit(solution)/shard_map/all_to_all | solution.py:67
  66.9 0.8 %fusion.3 = f32[32,8,128]{2,1,0:T(8,128)} fusion(bf16[32,8,128]{2,1,0:T(8,128)(2,1)S(1)} %all_to_all.21), kind=kLoop, calls=%fused_computation.6 | loop fusion | flops 196608 | bytes 196608 | tf_op jit(solution)/shard_map/mul | solution.py:91
Async XLA Ops:
  0.6 20.9 %all-to-all-start = ((f32[32,8,128]{2,1,0:T(8,128)}), f32[32,8,128]{2,1,0:T(8,128)S(1)}, u32[]{:S(2)}, u32[]{:S(2)}) async-start(f32[32,8,128]{2,1,0:T(8,128)} %param.4), calls=%async_computation | async-start | bytes 262144 | tf_op jit(solution)/shard_map/all_to_all | solution.py:67
  16.8 0.7 copy-start
  17.4 0.7 copy-start.1
  18.1 0.7 copy-start.2
  21.5 8.1 %collective-permute-start = (f32[256,128]{1,0:T(8,128)S(1)}, f32[256,128]{1,0:T(8,128)S(1)}, u32[]{:S(2)}, u32[]{:S(2)}) collective-permute-start(f32[256,128]{1,0:T(8,128)S(1)} %bitcast.2), channel_id=1, source_target_pairs={{1,0},{2,1},{3,2},{4,3},{5,4},{6,5},{7,6},{8,7},{9,8},{10,9},{11,1... | collective-permute-start | bytes 393224 | tf_op jit(solution)/shard_map/ppermute | solution.py:230
  25.2 25.7 %collective-permute-start.1 = (f32[256,128]{1,0:T(8,128)S(1)}, f32[256,128]{1,0:T(8,128)S(1)}, u32[]{:S(2)}, u32[]{:S(2)}) collective-permute-start(f32[256,128]{1,0:T(8,128)S(1)} %bitcast.3), channel_id=1, source_target_pairs={{0,1},{1,2},{2,3},{3,4},{4,5},{5,6},{6,7},{7,8},{8,9},{9,10},{10,1... | collective-permute-start | bytes 393224 | tf_op jit(solution)/shard_map/ppermute | solution.py:232
  42.7 10.6 %all-to-all-start.2 = ((f32[16,1,128]{2,1,0:T(1,128)}), f32[16,1,128]{2,1,0:T(1,128)S(1)}, u32[]{:S(2)}, u32[]{:S(2)}) async-start(f32[16,1,128]{2,1,0:T(1,128)} %regroup.1), calls=%async_computation.2 | async-start | bytes 16384 | tf_op jit(solution)/shard_map/all_to_all | solution.py:67
